TPU v7x, 512 devices: a whole 4x8x8 slice. The times are simulated.
512 devices in a mesh: vis: 64 (over y, z), chan: 8 (over x, core).
Axes of the slice: x: 4, y: 8, z: 8, core: 2. Of those that a mesh axis runs over, the one named last changes fastest.
Arguments:
- model: float32 [2, 256, 1024], P(None, 'vis', 'chan'), may hold values from -6 to 6
- kernels: float32 [2, 32, 8], replicated, may hold values from -1.5 to 1.5
- vis_data: float32 [2, 8, 524288], P(None, 'chan', 'vis'), may hold values from -6 to 6
- vis_weight: float32 [8, 524288], P('chan', 'vis'), may hold values from 0.2 to 2
- tile_list: int32 [8, 64, 16], P('chan', 'vis'), may hold values from 0 to 255, as said below
- vis_slot: int32 [8, 524288], P('chan', 'vis'), may hold values from 0 to 15
- vis_wplane: int32 [8, 524288], P('chan', 'vis'), may hold values from 0 to 31
- vis_offset: int32 [2, 8, 524288], P(None, 'chan', 'vis'), may hold values from 0 to 24
Outputs:
- model_step: float32 [2, 256, 1024], P(None, 'vis', 'chan')
- residual: float32 [2, 8, 524288], P(None, 'chan', 'vis')
Inputs may be any that keep to these rules, and one draw needn't show every extreme that they name: `tile_list`: the 16 tiles of one block's list are different and have different owners t // 4.
All inputs are finite; a program needn't handle non-finite values.
Results may differ from a plain program's by a relative error of at most 0.0003.
Values sent between devices are 32-bit elements; how exact they have to be, the bound alone decides.
No kernel may reach another device: no remote copies, remote signals or barrier semaphores. Data moves between devices by JAX's collectives and lax.ppermute only.
A program may use at most 64 MiB of HBM per device.

v0:
```python
import math

import jax
import jax.numpy as jnp
from jax import lax
from jax.sharding import PartitionSpec as P

TILE_SIDE = 32


HIGH = lax.Precision.HIGHEST


def dft_tables(side):
    index = jnp.arange(side, dtype=jnp.int32)
    angle = 2.0 * math.pi / side * (index[:, None] * index[None, :] % side).astype(jnp.float32)
    scale = 1.0 / math.sqrt(side)
    return (jnp.cos(angle) * scale, -jnp.sin(angle) * scale)


def forward(images, cosine, sine):

    def triple(left, right):
        return jnp.einsum("pa,tab,bq->tqp", left, images, right, precision=HIGH)

    return (
        triple(cosine, cosine) - triple(sine, sine),
        triple(cosine, sine) + triple(sine, cosine),
    )


def adjoint(part_re, part_im, cosine, sine):

    def triple(left, middle, right):
        return jnp.einsum("ap,tqp,qb->tab", left, middle, right, precision=HIGH)

    return (
        triple(cosine, part_re, cosine)
        - triple(sine, part_re, sine)
        + triple(sine, part_im, cosine)
        + triple(cosine, part_im, sine)
    )


def place(offset, taps, side):
    rows = jnp.arange(side, dtype=jnp.int32)[:, None]
    shift = rows - offset[None, :]
    total = jnp.zeros((side, offset.shape[0]), jnp.float32)
    for tap in range(taps.shape[0]):
        total = total + jnp.where(shift == tap, taps[tap][None, :], jnp.float32(0.0))
    return total


def crossed(left, right):
    return lax.dot_general(left, right, (((1,), (1,)), ((), ())), precision=HIGH)


def visibility_pass(
    grid_re, grid_im, slot, wplane, off_u, off_v, data_re, data_im, weight, kernels
):
    slots, side = (grid_re.shape[0], grid_re.shape[1])
    planes = kernels.shape[1]
    picker = (jnp.arange(planes, dtype=jnp.int32)[:, None] == wplane[None, :]).astype(jnp.float32)
    taps_re = jnp.dot(kernels[0].T, picker, precision=HIGH)
    taps_im = jnp.dot(kernels[1].T, picker, precision=HIGH)
    a_re = place(off_u, taps_re, side)
    a_im = place(off_u, taps_im, side)
    b_re = place(off_v, taps_re, side)
    b_im = place(off_v, taps_im, side)
    flat_re = grid_re.reshape(slots * side, side)
    flat_im = grid_im.reshape(slots * side, side)
    y_re = jnp.dot(flat_re, a_re, precision=HIGH) - jnp.dot(flat_im, a_im, precision=HIGH)
    y_im = jnp.dot(flat_re, a_im, precision=HIGH) + jnp.dot(flat_im, a_re, precision=HIGH)
    y_re = y_re.reshape(slots, side, -1)
    y_im = y_im.reshape(slots, side, -1)
    owner = (jnp.arange(slots, dtype=jnp.int32)[:, None] == slot[None, :]).astype(jnp.float32)
    pred_re = jnp.sum(owner * jnp.sum(y_re * b_re[None] - y_im * b_im[None], axis=1), axis=0)
    pred_im = jnp.sum(owner * jnp.sum(y_re * b_im[None] + y_im * b_re[None], axis=1), axis=0)
    res_re = weight * (data_re - pred_re)
    res_im = weight * (data_im - pred_im)
    z_re = (owner[:, None, :] * (res_re * b_re + res_im * b_im)[None]).reshape(slots * side, -1)
    z_im = (owner[:, None, :] * (res_im * b_re - res_re * b_im)[None]).reshape(slots * side, -1)
    part_re = crossed(z_re, a_re) + crossed(z_im, a_im)
    part_im = crossed(z_im, a_re) - crossed(z_re, a_im)
    return (res_re, res_im, part_re.reshape(slots, side, side), part_im.reshape(slots, side, side))


def shards(model, kernels, vis_data, vis_weight, tile_list, vis_slot, vis_wplane, vis_offset):
    side = TILE_SIDE
    cells = side * side
    channels = lax.axis_size("chan")
    chan_here = lax.axis_index("chan")
    offsets_all = (jnp.arange(channels, dtype=jnp.float32) - 0.5 * (channels - 1)) / channels
    frequency = jnp.sum(
        jnp.where(jnp.arange(channels, dtype=jnp.int32) == chan_here, offsets_all, jnp.float32(0.0))
    )
    cosine, sine = dft_tables(side)
    listed = tile_list[0, 0]
    slots = listed.shape[0]
    tile_dev = model.shape[1]
    piece_cells = model.shape[2]
    whole = lax.all_gather(model, "chan", axis=2, tiled=True)

    def matches(length):
        return (listed[:, None] == jnp.arange(length, dtype=jnp.int32)[None, :]).astype(jnp.float32)

    image = (whole[0] + frequency * whole[1]).reshape(tile_dev, side, side)
    own_re, own_im = forward(image, cosine, sine)
    packed = jnp.concatenate(
        [own_re.reshape(tile_dev, cells), own_im.reshape(tile_dev, cells)], axis=1
    )
    piece = lax.all_gather(packed, "vis", axis=0, tiled=True)
    chosen = jnp.dot(matches(piece.shape[0]), piece, precision=HIGH)
    grid_re = chosen[:, :cells].reshape(slots, side, side)
    grid_im = chosen[:, cells:].reshape(slots, side, side)
    count = vis_data.shape[2]
    block = min(512, count)
    blocks = count // block

    def rows_of(values):
        return values.reshape(blocks, block)

    sequence = (
        rows_of(vis_slot[0]),
        rows_of(vis_wplane[0]),
        rows_of(vis_offset[0, 0]),
        rows_of(vis_offset[1, 0]),
        rows_of(vis_data[0, 0]),
        rows_of(vis_data[1, 0]),
        rows_of(vis_weight[0]),
    )

    def one_block(carry, inputs):
        slot, wplane, off_u, off_v, data_re, data_im, weight = inputs
        res_re, res_im, part_re, part_im = visibility_pass(
            grid_re, grid_im, slot, wplane, off_u, off_v, data_re, data_im, weight, kernels
        )
        return ((carry[0] + part_re, carry[1] + part_im), (res_re, res_im))

    empty = jnp.zeros((slots, side, side), jnp.float32)
    (acc_re, acc_im), (out_re, out_im) = lax.scan(one_block, (empty, empty), sequence)
    residual = jnp.stack([out_re.reshape(count), out_im.reshape(count)])[:, None, :]
    partial_tiles = jnp.concatenate(
        [acc_re.reshape(slots, cells), acc_im.reshape(slots, cells)], axis=1
    )
    owned = lax.psum_scatter(
        jnp.dot(matches(lax.axis_size("vis") * tile_dev).T, partial_tiles, precision=HIGH),
        "vis",
        scatter_dimension=0,
        tiled=True,
    )
    dirty = adjoint(
        owned[:, :cells].reshape(tile_dev, side, side),
        owned[:, cells:].reshape(tile_dev, side, side),
        cosine,
        sine,
    ).reshape(tile_dev, cells)
    every = lax.all_gather(dirty[None], "chan", axis=0, tiled=True)
    mine = lax.dynamic_slice_in_dim(every, chan_here * piece_cells, piece_cells, 2)
    gradient = jnp.stack(
        [jnp.sum(mine, axis=0), jnp.sum(offsets_all[:, None, None] * mine, axis=0)]
    )
    curvature = jnp.stack([jnp.float32(channels), jnp.sum(offsets_all * offsets_all)])
    model_step = gradient / curvature[:, None, None]
    return (model_step, residual)


def solution(mesh):
    placed = (
        P(None, "vis", "chan"),
        P(),
        P(None, "chan", "vis"),
        P("chan", "vis"),
        P("chan", "vis", None),
        P("chan", "vis"),
        P("chan", "vis"),
        P(None, "chan", "vis"),
    )
    return jax.shard_map(
        shards,
        mesh=mesh,
        in_specs=placed,
        out_specs=(P(None, "vis", "chan"), P(None, "chan", "vis")),
        check_vma=False,
    )
```

profile of v0, /device:TPU:1, one launch (start us, length us, event | category | flops | bytes accessed | tf_op | source)
XLA Modules:
  0.0 474.5 jit_solution(9715506819741355807)
XLA Ops:
  7.9 18.1 %all_gather.9 = f32[2,4,1024]{2,1,0:T(4,128)S(1)} all-gather(f32[2,4,128]{2,1,0:T(4,128)} %param.10), channel_id=1, replica_groups=mesh['vis'=64,'chan'=8] {'chan'}, dimensions={2}, use_global_device_ids=true | all-gather | bytes 36864 | tf_op jit(solution)/shard_map/all_gather | solution.py:102
  34.6 73.3 %all-gather.3.cloned.1.call-done = f32[64,4,2048]{2,1,0:T(4,128)} async-done(((f32[1,4,2048]{2,1,0:T(4,128)}), f32[64,4,2048]{2,1,0:T(4,128)}) %all-gather.3.cloned.1.call-update) | async-done | bytes 2097168 | tf_op jit(solution)/shard_map/all_gather | solution.py:112
  107.9 2.0 reshape.1041
  110.7 171.5 %while.17 = (s32[]{:T(128)}, f32[16,32,32]{1,0,2:T(8,128)S(1)}, f32[16,32,32]{1,0,2:T(8,128)S(1)}, f32[16,512]{1,0:T(8,128)S(1)}, f32[16,512]{1,0:T(8,128)S(1)},...) while((s32[]{:T(128)}, f32[16,32,32]{1,0,2:T(8,128)S(1)}, ...), condition=%wide.region_6.7_spmd.clone, body=%wide.region_1.6_spmd.clone.sunk | while | flops 816292864 | bytes 15255747 | solution.py:141
  114.6 1.4 subtract_reduce_fusion.2
  125.3 1.4 subtract_reduce_fusion.2
  136.0 1.4 subtract_reduce_fusion.2
  146.8 1.4 subtract_reduce_fusion.2
  157.5 1.4 subtract_reduce_fusion.2
  168.2 1.4 subtract_reduce_fusion.2
  178.9 1.4 subtract_reduce_fusion.2
  189.6 1.4 subtract_reduce_fusion.2
  200.4 1.4 subtract_reduce_fusion.2
  211.1 1.4 subtract_reduce_fusion.2
  221.8 1.4 subtract_reduce_fusion.2
  232.5 1.4 subtract_reduce_fusion.2
  243.2 1.4 subtract_reduce_fusion.2
  254.0 1.4 subtract_reduce_fusion.2
  264.7 1.4 subtract_reduce_fusion.2
  275.4 1.4 subtract_reduce_fusion.2
  282.9 2.4 fusion.101
  285.3 1.3 dynamic-slice
  289.6 156.2 %all-reduce.3.cloned.1.call-done = f32[256,2048]{1,0:T(8,128)} async-done(((f32[256,2048]{1,0:T(8,128)}), f32[256,2048]{1,0:T(8,128)}) %all-reduce.3.cloned.1.call-update) | async-done | bytes 2097168
  449.8 17.2 %all_gather.11 = f32[8,4,1024]{2,1,0:T(4,128)S(1)} all-gather(f32[1,4,1024]{2,1,0:T(4,128)S(1)} %broadcast_in_dim_reshape.3), channel_id=1, replica_groups=mesh['vis'=64,'chan'=8] {'chan'}, dimensions={0}, use_global_device_ids=true | all-gather | bytes 147456 | tf_op jit(solution)/shard_map/all_gather | solution.py:158
  (521 shorter events, 163.3 us)
Async XLA Ops:
  7.2 24.8 %copy-start.1 = (s32[1,8192]{1,0:T(1,128)S(1)}, s32[1,8192]{1,0:T(1,128)}, u32[]{:S(2)}) copy-start(s32[1,8192]{1,0:T(1,128)} %param.15) | copy-start | bytes 98308
  7.2 25.5 %copy-start.2 = (s32[1,8192]{1,0:T(1,128)S(1)}, s32[1,8192]{1,0:T(1,128)}, u32[]{:S(2)}) copy-start(s32[1,8192]{1,0:T(1,128)} %param.16) | copy-start | bytes 98308
  7.2 26.7 %copy-start.3 = (f32[1,8192]{1,0:T(1,128)S(1)}, f32[1,8192]{1,0:T(1,128)}, u32[]{:S(2)}) copy-start(f32[1,8192]{1,0:T(1,128)} %param.13) | copy-start | bytes 98308
  7.2 100.7 %all-gather.3.cloned.1.call-start = ((), (), s32[]{:S(2)}) async-start(), calls=%async_computation | async-start | bytes 2129920 | tf_op jit(solution)/shard_map/all_gather | solution.py:112
  29.4 416.4 %all-reduce.3.cloned.1.call-start = ((), (), s32[]{:S(2)}) async-start(), calls=%async_computation.1 | async-start | bytes 4194304
  34.6 75.3 %copy-start.4 = (s32[1,1,16]{2,1,0:T(1,128)S(1)}, s32[1,1,16]{2,1,0:T(1,128)}, u32[]{:S(2)}) copy-start(s32[1,1,16]{2,1,0:T(1,128)} %param.14) | copy-start | bytes 196
  109.9 0.9 copy-start
Sparse Core Ops, SparseCore 0:
  29.5 78.3 all-gather.2
  285.4 160.3 all-reduce.2
where the time goes:
time: 475 us
  waiting for transfers between devices  230 us (48%)
  matrix products  155 us (33%)
  blocking collectives  35.3 us (7%)
  local copies, waits for them, and re-layouts  19.6 us (4%)
  other arithmetic  16.9 us (4%)
  between operations  15 us (3%)
    unnamed x3, waiting for transfers between devices  156 us
    all_gather x1, waiting for transfers between devices, shards(): piece = lax.all_gather(packed, 'vis', axis=0, tiled=True)  73.3 us
    dot_general x64, matrix products, crossed(): lax.dot_general(left, right, (((1,), (1,)), ((), ())), precision=HIGH)  70.7 us
    dot_general x16, matrix products, visibility_pass(): jnp.dot(flat_im, a_re, precision=HIGH)  22.7 us
    all_gather x1, blocking collectives, shards(): whole = lax.all_gather(model, 'chan', axis=2, tiled=True)  18.1 us
    all_gather x1, blocking collectives, shards(): every = lax.all_gather(dirty[None], 'chan', axis=0, tiled=True)  17.2 us
    dot_general x16, matrix products, visibility_pass(): jnp.dot(flat_im, a_im, precision=HIGH)  16.9 us
    dot_general x16, matrix products, visibility_pass(): jnp.dot(flat_re, a_re, precision=HIGH)  16.4 us
  transfers between devices with their start and end apart: 2, of which 2 were waited for; matrix products, arithmetic and copies ran while one was open for 2% of the time, Pallas kernels for 0%

commit v1 on v0

v1 whole, which is shorter than its diff:
```python
import math

import jax
import jax.numpy as jnp
import numpy as np
from jax import lax
from jax.experimental import pallas as pl
from jax.experimental.pallas import tpu as pltpu
from jax.sharding import PartitionSpec as P

SIDE = 32
LANES = 128
SLOTS = 16
OWNERS = 64
CHANS = 8
WITHIN = 4
CHUNK = 256
UNROLL = 2

F32 = jnp.float32
BF16 = jnp.bfloat16


def phase_tables():
    index = np.arange(SIDE)
    turn = np.zeros((SIDE, LANES), np.int64)
    turn[:, :SIDE] = index[:, None] * index[None, :] % SIDE
    angle = 2.0 * np.pi / SIDE * turn
    return np.stack([np.cos(angle), -np.sin(angle)]).astype(np.float32)


def split(x):
    high = x.astype(BF16)
    return high, (x - high.astype(F32)).astype(BF16)


def visibility_kernel(
    image_ref, taps_ref, phase_ref, slot_ref, plane_ref, offset_ref, data_ref, weight_ref,
    residual_ref, dirty_ref, grid_ref, total_ref, table_ref,
):
    rows = slot_ref.shape[0]
    scale = 1.0 / math.sqrt(SIDE)
    cos_s = phase_ref[0][:, :8] * scale
    sin_s = phase_ref[1][:, :8] * scale

    def tapped(table, taps):
        return lax.dot_general(
            table, taps, (((1,), (1,)), ((), ())),
            precision=lax.Precision.HIGHEST, preferred_element_type=F32,
        )

    k_re = tapped(cos_s, taps_ref[0]) - tapped(sin_s, taps_ref[1])
    k_im = tapped(cos_s, taps_ref[1]) + tapped(sin_s, taps_ref[0])
    table_ref[0] = jnp.concatenate([k_re] * 4, axis=1)
    table_ref[1] = jnp.concatenate([k_im] * 4, axis=1)

    for low in range(4):
        tiles = [image_ref[pl.ds(high * 4 + low, 8, stride=SLOTS), :] for high in range(4)]
        for step in range(4):
            grid_ref[pl.ds(low * SIDE + step, 8, stride=4), :] = jnp.concatenate(
                [t[:, step * SIDE : (step + 1) * SIDE] for t in tiles], axis=1
            )
    turned = grid_ref[...].T
    t_high, t_low = split(turned)
    left = jnp.concatenate(
        [jnp.concatenate([t_high, t_high], axis=1), jnp.concatenate([t_low, t_low], axis=1)],
        axis=0,
    )
    total_ref[...] = jnp.zeros_like(total_ref)

    def spread(x, masks):
        high, low = split(x)
        return jnp.concatenate([high * m for m in masks] + [low * m for m in masks], axis=0)

    def masks_of(part):
        return [
            jnp.broadcast_to(jnp.where(part == k, F32(1), F32(0)), (SIDE, LANES)).astype(BF16)
            for k in range(4)
        ]

    def take(table, index):
        return jnp.take_along_axis(table, index, axis=1, mode="promise_in_bounds")

    per_chunk = CHUNK // LANES

    def one_chunk(first):
        lefts_re, lefts_im, rights, masks_high, highs = [], [], [], [], []
        for t in range(per_chunk):
            row = first + t
            slot = slot_ref[pl.ds(row, 1), :]
            plane = jnp.broadcast_to(plane_ref[pl.ds(row, 1), :], (SIDE, LANES))
            u0 = jnp.broadcast_to(offset_ref[0, pl.ds(row, 1), :], (SIDE, LANES))
            v0 = jnp.broadcast_to(offset_ref[1, pl.ds(row, 1), :], (SIDE, LANES))
            w_re, w_im = take(table_ref[0], plane), take(table_ref[1], plane)
            e_re, e_im = take(phase_ref[0], u0), take(phase_ref[1], u0)
            f_re, f_im = take(phase_ref[0], v0), take(phase_ref[1], v0)
            low_masks = masks_of(slot & 3)
            high = slot >> 2
            lefts_re.append(spread(w_re * e_re - w_im * e_im, low_masks))
            lefts_im.append(spread(w_re * e_im + w_im * e_re, low_masks))
            rights.append((w_re * f_re - w_im * f_im, w_re * f_im + w_im * f_re))
            highs.append(jnp.broadcast_to(high, (SIDE, LANES)))
            masks_high.append(masks_of(high))
        a_re = jnp.concatenate(lefts_re, axis=1)
        a_im = jnp.concatenate(lefts_im, axis=1)
        y_re = jnp.dot(left, a_re, preferred_element_type=F32)
        y_im = jnp.dot(left, a_im, preferred_element_type=F32)

        def chosen(y, t):
            y = y[:, t * LANES : (t + 1) * LANES]
            y = y[: 4 * SIDE] + y[4 * SIDE :]
            parts = [y[k * SIDE : (k + 1) * SIDE] for k in range(4)]
            upper = jnp.where(highs[t] == 3, parts[3], parts[2])
            lower = jnp.where(highs[t] == 1, parts[1], parts[0])
            return jnp.where(highs[t] >= 2, upper, lower)

        z_re_all, z_im_all = [], []
        for t in range(per_chunk):
            row = first + t
            b_re, b_im = rights[t]
            p_re, p_im = chosen(y_re, t), chosen(y_im, t)
            pred_re = jnp.sum(p_re * b_re - p_im * b_im, axis=0, keepdims=True)
            pred_im = jnp.sum(p_re * b_im + p_im * b_re, axis=0, keepdims=True)
            weight = weight_ref[pl.ds(row, 1), :]
            r_re = weight * (data_ref[0, pl.ds(row, 1), :] - pred_re)
            r_im = weight * (data_ref[1, pl.ds(row, 1), :] - pred_im)
            residual_ref[0, pl.ds(row, 1), :] = r_re
            residual_ref[1, pl.ds(row, 1), :] = r_im
            z_re_all.append(spread(r_re * b_re + r_im * b_im, masks_high[t]))
            z_im_all.append(spread(r_im * b_re - r_re * b_im, masks_high[t]))

        def crossed(x, y):
            return lax.dot_general(
                x, y, (((1,), (1,)), ((), ())), preferred_element_type=F32
            )

        return crossed(a_re, jnp.concatenate(z_re_all, axis=1)) + crossed(
            a_im, jnp.concatenate(z_im_all, axis=1)
        )

    def step(i, _):
        part = None
        for k in range(UNROLL):
            more = one_chunk((i * UNROLL + k) * per_chunk)
            part = more if part is None else part + more
        total_ref[...] += part
        return 0

    lax.fori_loop(0, rows // (per_chunk * UNROLL), step, 0)

    total = total_ref[...]
    total = total[:, : 4 * SIDE] + total[:, 4 * SIDE :]
    grid_ref[...] = total[: 4 * SIDE] + total[4 * SIDE :]
    for low in range(4):
        parts = [grid_ref[pl.ds(low * SIDE + s, 8, stride=4), :] for s in range(4)]
        for high in range(4):
            dirty_ref[pl.ds(high * 4 + low, 8, stride=SLOTS), :] = jnp.concatenate(
                [p[:, high * SIDE : (high + 1) * SIDE] for p in parts], axis=1
            )


def visibilities(image, kernels, slot, plane, offset, data, weight):
    rows = slot.shape[0]
    return pl.pallas_call(
        visibility_kernel,
        out_shape=(
            jax.ShapeDtypeStruct((2, rows, LANES), F32),
            jax.ShapeDtypeStruct((CHANS * SLOTS, LANES), F32),
        ),
        in_specs=[pl.BlockSpec(memory_space=pltpu.VMEM)] * 8,
        out_specs=(pl.BlockSpec(memory_space=pltpu.VMEM),) * 2,
        scratch_shapes=[
            pltpu.VMEM((LANES, LANES), F32),
            pltpu.VMEM((2 * LANES, 2 * LANES), F32),
            pltpu.VMEM((2, SIDE, LANES), F32),
        ],
        compiler_params=pltpu.CompilerParams(vmem_limit_bytes=32 * 1024 * 1024),
        name="visibilities",
    )(image, kernels, jnp.asarray(phase_tables()), slot, plane, offset, data, weight)


def frequency(channel):
    return (channel.astype(F32) - 0.5 * (CHANS - 1)) / CHANS


def select_kernel(list_ref, model_ref, image_ref):
    for channel in range(CHANS):
        offset = (channel - 0.5 * (CHANS - 1)) / CHANS
        for slot in range(SLOTS):
            tile = list_ref[channel, slot]
            first = (tile // WITHIN) * (2 * WITHIN) + tile % WITHIN
            image_ref[pl.ds(channel * SLOTS + slot, 1), :] = model_ref[
                pl.ds(first, 1), :
            ] + offset * model_ref[pl.ds(first + WITHIN, 1), :]


def select(listed, model):
    return pl.pallas_call(
        select_kernel,
        out_shape=jax.ShapeDtypeStruct((CHANS * SLOTS, LANES), F32),
        in_specs=[
            pl.BlockSpec(memory_space=pltpu.SMEM),
            pl.BlockSpec(memory_space=pltpu.VMEM),
        ],
        out_specs=pl.BlockSpec(memory_space=pltpu.VMEM),
        name="select",
    )(listed, model)


def collect_kernel(list_ref, dirty_ref, owned_ref):
    owned_ref[...] = jnp.zeros_like(owned_ref)
    for channel in range(CHANS):
        offset = (channel - 0.5 * (CHANS - 1)) / CHANS
        for slot in range(SLOTS):
            tile = list_ref[channel, slot]
            first = (tile // WITHIN) * (2 * WITHIN) + tile % WITHIN
            row = dirty_ref[pl.ds(channel * SLOTS + slot, 1), :]
            owned_ref[pl.ds(first, 1), :] += row
            owned_ref[pl.ds(first + WITHIN, 1), :] += offset * row


def collect(listed, dirty):
    return pl.pallas_call(
        collect_kernel,
        out_shape=jax.ShapeDtypeStruct((OWNERS * 2 * WITHIN, LANES), F32),
        in_specs=[
            pl.BlockSpec(memory_space=pltpu.SMEM),
            pl.BlockSpec(memory_space=pltpu.VMEM),
        ],
        out_specs=pl.BlockSpec(memory_space=pltpu.VMEM),
        name="collect",
    )(listed, dirty)


def shards(model, kernels, vis_data, vis_weight, tile_list, vis_slot, vis_wplane, vis_offset):
    count = vis_weight.shape[1]
    rows = count // LANES
    with jax.named_scope("lists"):
        listed = lax.all_to_all(
            jnp.broadcast_to(tile_list.reshape(1, SLOTS), (CHANS, SLOTS)),
            "chan", 0, 0, tiled=True,
        )
    with jax.named_scope("spread_model"):
        own = model.reshape(1, 2 * WITHIN, LANES)
        every = lax.all_to_all(
            jnp.broadcast_to(own, (OWNERS, 2 * WITHIN, LANES)), "vis", 0, 0, tiled=True
        )
    chosen = select(listed, every.reshape(OWNERS * 2 * WITHIN, LANES))
    with jax.named_scope("images"):
        image = lax.all_to_all(chosen, "chan", 0, 0, tiled=True)
    residual, dirty = visibilities(
        image,
        kernels,
        vis_slot.reshape(rows, LANES),
        vis_wplane.reshape(rows, LANES),
        vis_offset.reshape(2, rows, LANES),
        vis_data.reshape(2, rows, LANES),
        vis_weight.reshape(rows, LANES),
    )
    with jax.named_scope("dirty_cells"):
        pieces = lax.all_to_all(dirty, "chan", 0, 0, tiled=True)
    owned = collect(listed, pieces)
    with jax.named_scope("owners"):
        summed = lax.all_to_all(
            owned.reshape(OWNERS, 2 * WITHIN, LANES), "vis", 0, 0, tiled=True
        )
    gradient = jnp.sum(summed, axis=0).reshape(2, WITHIN, LANES)
    offsets = (np.arange(CHANS) - 0.5 * (CHANS - 1)) / CHANS
    curvature = np.array([CHANS, np.sum(offsets * offsets)], np.float32)
    model_step = gradient / curvature[:, None, None]
    return (model_step, residual.reshape(2, 1, count))


def solution(mesh):
    placed = (
        P(None, "vis", "chan"),
        P(),
        P(None, "chan", "vis"),
        P("chan", "vis"),
        P("chan", "vis", None),
        P("chan", "vis"),
        P("chan", "vis"),
        P(None, "chan", "vis"),
    )
    return jax.shard_map(
        shards,
        mesh=mesh,
        in_specs=placed,
        out_specs=(P(None, "vis", "chan"), P(None, "chan", "vis")),
        check_vma=False,
    )
```

time: 475 us -> 104 us (0.22)
  waiting for transfers between devices: 230 us -> 4.79 us
  matrix products: 155 us -> 0 us
  blocking collectives: 35.3 us -> 65.2 us
  Pallas kernels: 0 us -> 23.4 us
  local copies, waits for them, and re-layouts: 19.6 us -> 1.43 us
  other arithmetic: 16.9 us -> 0.73 us
  between operations: 15 us -> 0.69 us
  starting transfers between devices: 0.08 us -> 6.94 us
    unnamed x3 -> x0, waiting for transfers between devices: 156 us -> none
    dot_general x176 -> x0, matrix products: 155 us -> none  [the longest x64 70.7 us: crossed(): lax.dot_general(left, right, (((1,), (1,)), ((), ())), precision=HIGH)]
    all_gather x1 -> x0, waiting for transfers between devices: 73.3 us -> none  [shards(): piece = lax.all_gather(packed, 'vis', axis=0, tiled=True)]
    all_to_all x0 -> x4, blocking collectives: none -> 65.2 us  [the longest x1 24.5 us: shards(): lax.all_to_all(jnp.broadcast_to(own, (OWNERS, 2 * WITHIN, LANES)), 'vis',...]
    all_gather x2 -> x0, blocking collectives: 35.3 us -> none  [the longest x1 18.1 us: shards(): whole = lax.all_gather(model, 'chan', axis=2, tiled=True)]
    pallas_call x0 -> x3, Pallas kernels: none -> 23.4 us  [the longest x1 18.7 us: visibilities(): pl.pallas_call(visibility_kernel, out_shape=(jax.ShapeDtypeStruct((2, row...]
    all_to_all x0 -> x1, starting transfers between devices: none -> 6.94 us  [shards(): image = lax.all_to_all(chosen, 'chan', 0, 0, tiled=True)]
    all_to_all x0 -> x1, waiting for transfers between devices: none -> 4.79 us  [shards(): image = lax.all_to_all(chosen, 'chan', 0, 0, tiled=True)]
  transfers between devices with their start and end apart: 2 -> 1, of which waited for: 2 -> 1; matrix products, arithmetic and copies ran while one was open for 2% -> 0% of each run, Pallas kernels for 0% -> 0%
where the time goes in v1:
time: 104 us; the launch traced here: 103 us
  blocking collectives  65.2 us (63%)
  Pallas kernels  23.4 us (22%)
  starting transfers between devices  6.94 us (7%)
  waiting for transfers between devices  4.79 us (5%)
  local copies, waits for them, and re-layouts  1.43 us (1%)
    all_to_all x1, blocking collectives, shards(): lax.all_to_all(jnp.broadcast_to(own, (OWNERS, 2 * WITHIN, LANES)), 'vis',...  24.5 us
    pallas_call x1, Pallas kernels, visibilities(): pl.pallas_call(visibility_kernel, out_shape=(jax.ShapeDtypeStruct((2, row...  18.7 us
    all_to_all x1, blocking collectives, shards(): lax.all_to_all(owned.reshape(OWNERS, 2 * WITHIN, LANES), 'vis', 0, 0, til...  17.7 us
    all_to_all x1, blocking collectives, shards(): lax.all_to_all(jnp.broadcast_to(tile_list.reshape(1, SLOTS), (CHANS, SLOT...  14.4 us
    all_to_all x1, blocking collectives, shards(): pieces = lax.all_to_all(dirty, 'chan', 0, 0, tiled=True)  8.67 us
    all_to_all x1, starting transfers between devices, shards(): image = lax.all_to_all(chosen, 'chan', 0, 0, tiled=True)  6.94 us
    all_to_all x1, waiting for transfers between devices, shards(): image = lax.all_to_all(chosen, 'chan', 0, 0, tiled=True)  4.79 us
    pallas_call x1, Pallas kernels, select(): pl.pallas_call(select_kernel, out_shape=jax.ShapeDtypeStruct((CHANS * SLO...  2.4 us
  transfers between devices with their start and end apart: 1, of which 1 were waited for; matrix products, arithmetic and copies ran while one was open for 0% of the time, Pallas kernels for 0%

profile of v1, /device:TPU:1, one launch (start us, length us, event | category | flops | bytes accessed | tf_op | source)
XLA Modules:
  0.0 103.3 jit_solution(15112513728361141298)
XLA Ops:
  0.6 0.0 copy-start.8
  0.6 0.6 copy-done.8
  1.3 0.0 copy-start.7
  1.3 14.4 %all_to_all.40 = s32[8,1,16]{2,1,0:T(1,128)} all-to-all(s32[8,1,16]{2,1,0:T(1,128)S(1)} %broadcast_in_dim.12), channel_id=1, replica_groups=mesh['vis'=64,'chan'=8] {'chan'}, dimensions={0} | all-to-all | bytes 1024 | tf_op jit(solution)/shard_map/lists/all_to_all | solution.py:239
  15.7 0.0 copy-done.7
  15.7 24.5 %all_to_all.41 = f32[64,8,128]{2,1,0:T(8,128)} all-to-all(f32[64,8,128]{2,1,0:T(8,128)S(1)} %broadcast_in_dim.14), channel_id=1, replica_groups=mesh['vis'=64,'chan'=8] {'vis'}, dimensions={0} | all-to-all | bytes 524288 | tf_op jit(solution)/shard_map/spread_model/all_to_all | solution.py:245
  40.2 2.4 %select.1 = f32[128,128]{1,0:T(8,128)} custom-call(s32[8,16]{1,0:T(8,128)} %bitcast.27, f32[512,128]{1,0:T(8,128)} %bitcast.24), custom_call_target="tpu_custom_call" | custom-call | tf_op jit(solution)/shard_map/select/pallas_call | solution.py:198
  42.6 6.9 %all-to-all-start.2 = ((f32[8,16,128]{2,1,0:T(8,128)}), f32[8,16,128]{2,1,0:T(8,128)S(1)}, u32[]{:S(2)}, u32[]{:S(2)}) async-start(f32[8,16,128]{2,1,0:T(8,128)} %bitcast.25), calls=%async_computation.2 | async-start | bytes 131072 | tf_op jit(solution)/shard_map/images/all_to_all | solution.py:250
  49.6 0.0 copy-done.6
  49.6 0.1 copy.14.taps_ref
  49.6 4.8 %all-to-all-done.2 = f32[8,16,128]{2,1,0:T(8,128)S(1)} async-done(((f32[8,16,128]{2,1,0:T(8,128)}), f32[8,16,128]{2,1,0:T(8,128)S(1)}, u32[]{:S(2)}, u32[]{:S(2)}) %all-to-all-start.2) | async-done | bytes 65568 | tf_op jit(solution)/shard_map/images/all_to_all | solution.py:250
  54.4 0.0 copy-done.3
  54.4 0.0 copy-done.4
  54.4 0.0 copy-done.5
  54.4 0.0 copy-done
  54.4 0.0 copy-done.1
  54.5 0.0 copy-done.2
  54.5 18.7 %visibilities.1 = (f32[2,64,128]{2,1,0:T(8,128)}, f32[128,128]{1,0:T(8,128)S(1)}) custom-call(f32[128,128]{1,0:T(8,128)S(1)} %bitcast.16, f32[2,32,8]{2,1,0:T(8,128)S(1)} %copy.14.taps_ref, f32[2,32,128]{2,1,0:T(8,128)S(1)} %copy-done.5, s32[64,128]{1,0:T(8,128)S(1)} %bitcast.20, s32[64,128]{1,0:T(8,128)S(1)} %bitcast.21, s32[2,64,128]{2,1,0:T(8,128)S(1)} %bitcast.18, ...), custom_call_target="tpu_custom_call" | custom-call | tf_op jit(solution)/shard_map/visibilities/pallas_call | solution.py:164
  73.2 8.7 %all_to_all.42 = f32[8,16,128]{2,1,0:T(8,128)} all-to-all(f32[8,16,128]{2,1,0:T(8,128)S(1)} %bitcast.17), channel_id=1, replica_groups=mesh['vis'=64,'chan'=8] {'chan'}, dimensions={0} | all-to-all | bytes 131072 | tf_op jit(solution)/shard_map/dirty_cells/all_to_all | solution.py:261
  81.8 2.3 %collect.1 = f32[512,128]{1,0:T(8,128)} custom-call(s32[8,16]{1,0:T(8,128)} %bitcast.28, f32[128,128]{1,0:T(8,128)} %bitcast.26), custom_call_target="tpu_custom_call" | custom-call | tf_op jit(solution)/shard_map/collect/pallas_call | solution.py:223
  84.2 17.7 %all_to_all.43 = f32[64,8,128]{2,1,0:T(8,128)S(1)} all-to-all(f32[64,8,128]{2,1,0:T(8,128)} %bitcast.23), channel_id=1, replica_groups=mesh['vis'=64,'chan'=8] {'vis'}, dimensions={0} | all-to-all | bytes 524288 | tf_op jit(solution)/shard_map/owners/all_to_all | solution.py:264
  101.9 0.1 reduce_sum.9
  101.9 0.6 copy-done.9
  102.6 0.7 broadcast_multiply_fusion
  (10 shorter events, 0.0 us)
Async XLA Ops:
  0.6 0.7 copy-start.8
  1.3 14.4 %copy-start.7 = (f32[2,4,128]{2,1,0:T(4,128)S(1)}, f32[2,4,128]{2,1,0:T(4,128)}, u32[]{:S(2)}) copy-start(f32[2,4,128]{2,1,0:T(4,128)} %param.10) | copy-start | bytes 12292
  40.2 9.4 %copy-start.6 = (f32[2,32,8]{1,2,0:T(8,128)S(1)}, f32[2,32,8]{1,2,0:T(8,128)}, u32[]{:S(2)}) copy-start(f32[2,32,8]{1,2,0:T(8,128)} %param.11) | copy-start | bytes 6148
  40.2 14.2 %copy-start.3 = (s32[1,8192]{1,0:T(1,128)S(1)}, s32[1,8192]{1,0:T(1,128)}, u32[]{:S(2)}) copy-start(s32[1,8192]{1,0:T(1,128)} %param.16) | copy-start | bytes 98308
  40.2 14.2 %copy-start.4 = (f32[1,8192]{1,0:T(1,128)S(1)}, f32[1,8192]{1,0:T(1,128)}, u32[]{:S(2)}) copy-start(f32[1,8192]{1,0:T(1,128)} %param.13) | copy-start | bytes 98308
  40.2 14.2 %copy-start.5 = (f32[2,32,128]{2,1,0:T(8,128)S(1)}, f32[2,32,128]{2,1,0:T(8,128)}, u32[]{:S(2)}) copy-start(f32[2,32,128]{2,1,0:T(8,128)} %constant.6.clone.phase_ref) | copy-start | bytes 98308
  42.6 11.8 %copy-start = (s32[2,1,8192]{2,1,0:T(1,128)S(1)}, s32[2,1,8192]{2,1,0:T(1,128)}, u32[]{:S(2)}) copy-start(s32[2,1,8192]{2,1,0:T(1,128)} %param.17) | copy-start | bytes 196612
  42.6 11.8 %copy-start.1 = (f32[2,1,8192]{2,1,0:T(1,128)S(1)}, f32[2,1,8192]{2,1,0:T(1,128)}, u32[]{:S(2)}) copy-start(f32[2,1,8192]{2,1,0:T(1,128)} %param.12) | copy-start | bytes 196612
  42.6 11.8 %all-to-all-start.2 = ((f32[8,16,128]{2,1,0:T(8,128)}), f32[8,16,128]{2,1,0:T(8,128)S(1)}, u32[]{:S(2)}, u32[]{:S(2)}) async-start(f32[8,16,128]{2,1,0:T(8,128)} %bitcast.25), calls=%async_computation.2 | async-start | bytes 131072 | tf_op jit(solution)/shard_map/images/all_to_all | solution.py:250
  49.6 4.9 %copy-start.2 = (s32[1,8192]{1,0:T(1,128)S(1)}, s32[1,8192]{1,0:T(1,128)}, u32[]{:S(2)}) copy-start(s32[1,8192]{1,0:T(1,128)} %param.15) | copy-start | bytes 98308
  101.9 0.7 copy-start.9

commit v2 on v1

--- a/solution.py
+++ b/solution.py
@@ -14,8 +14,8 @@
 OWNERS = 64
 CHANS = 8
 WITHIN = 4
-CHUNK = 256
-UNROLL = 2
+CHUNK = 512
+UNROLL = 4
 
 F32 = jnp.float32
 BF16 = jnp.bfloat16
@@ -236,10 +236,7 @@
     count = vis_weight.shape[1]
     rows = count // LANES
     with jax.named_scope("lists"):
-        listed = lax.all_to_all(
-            jnp.broadcast_to(tile_list.reshape(1, SLOTS), (CHANS, SLOTS)),
-            "chan", 0, 0, tiled=True,
-        )
+        listed = lax.all_gather(tile_list.reshape(1, SLOTS), "chan", axis=0, tiled=True)
     with jax.named_scope("spread_model"):
         own = model.reshape(1, 2 * WITHIN, LANES)
         every = lax.all_to_all(
@@ -264,10 +261,10 @@
         summed = lax.all_to_all(
             owned.reshape(OWNERS, 2 * WITHIN, LANES), "vis", 0, 0, tiled=True
         )
-    gradient = jnp.sum(summed, axis=0).reshape(2, WITHIN, LANES)
     offsets = (np.arange(CHANS) - 0.5 * (CHANS - 1)) / CHANS
-    curvature = np.array([CHANS, np.sum(offsets * offsets)], np.float32)
-    model_step = gradient / curvature[:, None, None]
+    term = lax.broadcasted_iota(jnp.int32, (2, WITHIN, LANES), 0)
+    inverse = jnp.where(term == 0, F32(1.0 / CHANS), F32(1.0 / np.sum(offsets * offsets)))
+    model_step = jnp.sum(summed, axis=0).reshape(2, WITHIN, LANES) * inverse
     return (model_step, residual.reshape(2, 1, count))
 
 

time: 104 us -> 88.5 us (0.85)
  blocking collectives: 65.2 us -> 19.9 us
  starting transfers between devices: 6.94 us -> 32 us
  waiting for transfers between devices: 4.79 us -> 18.5 us
  Pallas kernels: 23.4 us -> 12.8 us
    all_to_all x3 -> x0, blocking collectives: 56.6 us -> none  [the longest x1 24.5 us: shards(): lax.all_to_all(jnp.broadcast_to(own, (OWNERS, 2 * WITHIN, LANES)), 'vis',...]
    all_to_all x0 -> x2, starting transfers between devices: none -> 24.2 us  [the longest x1 17.3 us: shards(): lax.all_to_all(jnp.broadcast_to(own, (OWNERS, 2 * WITHIN, LANES)), 'vis',...]
    all_to_all x0 -> x2, waiting for transfers between devices: none -> 13.7 us  [the longest x1 12.4 us: shards(): lax.all_to_all(owned.reshape(OWNERS, 2 * WITHIN, LANES), 'vis', 0, 0, til...]
    all_gather x0 -> x1, blocking collectives: none -> 11.2 us  [shards(): lax.all_gather(tile_list.reshape(1, SLOTS), 'chan', axis=0, tiled=True)]
    pallas_call x1, Pallas kernels: 18.7 us -> 8.11 us  [visibilities(): pl.pallas_call(visibility_kernel, out_shape=(jax.ShapeDtypeStruct((2, row...]
    broadcast_in_dim x1, local copies, waits for them, and re-layouts: 0.02 us -> 1.4 us  [shards(): jnp.broadcast_to(own, (OWNERS, 2 * WITHIN, LANES))]
  transfers between devices with their start and end apart: 1 -> 3, of which waited for: 1 -> 3; matrix products, arithmetic and copies ran while one was open for 0% -> 0% of each run, Pallas kernels for 0% -> 0%
where the time goes in v2:
time: 88.5 us; the launch traced here: 86.9 us
  starting transfers between devices  32 us (36%)
  blocking collectives  19.9 us (22%)
  waiting for transfers between devices  18.5 us (21%)
  Pallas kernels  12.8 us (14%)
  local copies, waits for them, and re-layouts  2.2 us (2%)
    all_to_all x1, starting transfers between devices, shards(): lax.all_to_all(jnp.broadcast_to(own, (OWNERS, 2 * WITHIN, LANES)), 'vis',...  17.3 us
    all_to_all x1, waiting for transfers between devices, shards(): lax.all_to_all(owned.reshape(OWNERS, 2 * WITHIN, LANES), 'vis', 0, 0, til...  12.4 us
    all_gather x1, blocking collectives, shards(): lax.all_gather(tile_list.reshape(1, SLOTS), 'chan', axis=0, tiled=True)  11.2 us
    all_to_all x1, blocking collectives, shards(): pieces = lax.all_to_all(dirty, 'chan', 0, 0, tiled=True)  8.66 us
    pallas_call x1, Pallas kernels, visibilities(): pl.pallas_call(visibility_kernel, out_shape=(jax.ShapeDtypeStruct((2, row...  8.11 us
    all_to_all x1, starting transfers between devices, shards(): image = lax.all_to_all(chosen, 'chan', 0, 0, tiled=True)  7.81 us
    all_to_all x1, starting transfers between devices, shards(): lax.all_to_all(owned.reshape(OWNERS, 2 * WITHIN, LANES), 'vis', 0, 0, til...  6.95 us
    all_to_all x1, waiting for transfers between devices, shards(): image = lax.all_to_all(chosen, 'chan', 0, 0, tiled=True)  4.77 us
  transfers between devices with their start and end apart: 3, of which 3 were waited for; matrix products, arithmetic and copies ran while one was open for 0% of the time, Pallas kernels for 0%

profile of v2, /device:TPU:1, one launch (start us, length us, event | category | flops | bytes accessed | tf_op | source)
XLA Modules:
  0.0 86.9 jit_solution(642836287335697775)
XLA Ops:
  0.6 1.4 %broadcast_in_dim.16 = f32[64,8,128]{2,1,0:T(8,128)} broadcast(f32[8,128]{1,0:T(8,128)} %bitcast.29), dimensions={1,2} | broadcast | bytes 266240 | tf_op jit(solution)/shard_map/spread_model/broadcast_in_dim | solution.py:243
  2.0 17.3 %all-to-all-start = ((f32[64,8,128]{2,1,0:T(8,128)}), f32[64,8,128]{2,1,0:T(8,128)S(1)}, u32[]{:S(2)}, u32[]{:S(2)}) async-start(f32[64,8,128]{2,1,0:T(8,128)} %broadcast_in_dim.16), calls=%async_computation | async-start | bytes 524288 | tf_op jit(solution)/shard_map/spread_model/all_to_all | solution.py:242
  19.3 0.0 copy-done.8
  19.3 11.2 %all-gather = s32[8,1,16]{2,1,0:T(1,128)} all-gather(s32[1,1,16]{2,1,0:T(1,128)S(1)} %copy-done.8), channel_id=2, replica_groups=mesh['vis'=64,'chan'=8] {'chan'}, dimensions={0}, use_global_device_ids=true | all-gather | bytes 576 | tf_op jit(solution)/shard_map/lists/all_gather | solution.py:239
  30.6 1.3 %all-to-all-done = f32[64,8,128]{2,1,0:T(8,128)S(1)} async-done(((f32[64,8,128]{2,1,0:T(8,128)}), f32[64,8,128]{2,1,0:T(8,128)S(1)}, u32[]{:S(2)}, u32[]{:S(2)}) %all-to-all-start) | async-done | bytes 262176 | tf_op jit(solution)/shard_map/spread_model/all_to_all | solution.py:242
  31.9 0.7 copy-done.6
  32.6 2.4 %select.1 = f32[128,128]{1,0:T(8,128)} custom-call(s32[8,16]{1,0:T(8,128)} %bitcast.26, f32[512,128]{1,0:T(8,128)} %bitcast.22), custom_call_target="tpu_custom_call" | custom-call | tf_op jit(solution)/shard_map/select/pallas_call | solution.py:198
  35.0 7.8 %all-to-all-start.1 = ((f32[8,16,128]{2,1,0:T(8,128)}), f32[8,16,128]{2,1,0:T(8,128)S(1)}, u32[]{:S(2)}, u32[]{:S(2)}) async-start(f32[8,16,128]{2,1,0:T(8,128)} %bitcast.24), calls=%async_computation.1 | async-start | bytes 131072 | tf_op jit(solution)/shard_map/images/all_to_all | solution.py:247
  42.8 0.0 copy-done.7
  42.8 0.1 copy.14.taps_ref
  42.9 4.8 %all-to-all-done.1 = f32[8,16,128]{2,1,0:T(8,128)S(1)} async-done(((f32[8,16,128]{2,1,0:T(8,128)}), f32[8,16,128]{2,1,0:T(8,128)S(1)}, u32[]{:S(2)}, u32[]{:S(2)}) %all-to-all-start.1) | async-done | bytes 65568 | tf_op jit(solution)/shard_map/images/all_to_all | solution.py:247
  47.6 0.0 copy-done.3
  47.6 0.0 copy-done.4
  47.6 0.0 copy-done.5
  47.7 0.0 copy-done
  47.7 0.0 copy-done.1
  47.7 0.0 copy-done.2
  47.7 8.1 %visibilities.1 = (f32[2,64,128]{2,1,0:T(8,128)}, f32[128,128]{1,0:T(8,128)S(1)}) custom-call(f32[128,128]{1,0:T(8,128)S(1)} %bitcast.15, f32[2,32,8]{2,1,0:T(8,128)S(1)} %copy.14.taps_ref, f32[2,32,128]{2,1,0:T(8,128)S(1)} %copy-done.5, s32[64,128]{1,0:T(8,128)S(1)} %bitcast.19, s32[64,128]{1,0:T(8,128)S(1)} %bitcast.20, s32[2,64,128]{2,1,0:T(8,128)S(1)} %bitcast.17, ...), custom_call_target="tpu_custom_call" | custom-call | tf_op jit(solution)/shard_map/visibilities/pallas_call | solution.py:164
  55.8 8.7 %all_to_all.32 = f32[8,16,128]{2,1,0:T(8,128)} all-to-all(f32[8,16,128]{2,1,0:T(8,128)S(1)} %bitcast.16), channel_id=1, replica_groups=mesh['vis'=64,'chan'=8] {'chan'}, dimensions={0} | all-to-all | bytes 131072 | tf_op jit(solution)/shard_map/dirty_cells/all_to_all | solution.py:258
  64.4 2.3 %collect.1 = f32[512,128]{1,0:T(8,128)} custom-call(s32[8,16]{1,0:T(8,128)} %bitcast.27, f32[128,128]{1,0:T(8,128)} %bitcast.25), custom_call_target="tpu_custom_call" | custom-call | tf_op jit(solution)/shard_map/collect/pallas_call | solution.py:223
  66.8 6.9 %all-to-all-start.3 = ((f32[64,8,128]{2,1,0:T(8,128)}), f32[64,8,128]{2,1,0:T(8,128)S(1)}, u32[]{:S(2)}, u32[]{:S(2)}) async-start(f32[64,8,128]{2,1,0:T(8,128)} %bitcast.23), calls=%async_computation.3 | async-start | bytes 524288 | tf_op jit(solution)/shard_map/owners/all_to_all | solution.py:261
  73.7 12.4 %all-to-all-done.3 = f32[64,8,128]{2,1,0:T(8,128)S(1)} async-done(((f32[64,8,128]{2,1,0:T(8,128)}), f32[64,8,128]{2,1,0:T(8,128)S(1)}, u32[]{:S(2)}, u32[]{:S(2)}) %all-to-all-start.3) | async-done | bytes 262176 | tf_op jit(solution)/shard_map/owners/all_to_all | solution.py:261
  86.2 0.1 reduce_sum.9
  86.2 0.7 broadcast_multiply_fusion
  (10 shorter events, 0.0 us)
Async XLA Ops:
  2.0 17.3 %copy-start.8 = (s32[1,1,16]{2,1,0:T(1,128)S(1)}, s32[1,1,16]{2,1,0:T(1,128)}, u32[]{:S(2)}) copy-start(s32[1,1,16]{2,1,0:T(1,128)} %param.13) | copy-start | bytes 196
  2.0 29.8 %all-to-all-start = ((f32[64,8,128]{2,1,0:T(8,128)}), f32[64,8,128]{2,1,0:T(8,128)S(1)}, u32[]{:S(2)}, u32[]{:S(2)}) async-start(f32[64,8,128]{2,1,0:T(8,128)} %broadcast_in_dim.16), calls=%async_computation | async-start | bytes 524288 | tf_op jit(solution)/shard_map/spread_model/all_to_all | solution.py:242
  31.9 0.7 copy-start.6
  32.6 10.2 %copy-start.7 = (f32[2,32,8]{1,2,0:T(8,128)S(1)}, f32[2,32,8]{1,2,0:T(8,128)}, u32[]{:S(2)}) copy-start(f32[2,32,8]{1,2,0:T(8,128)} %param.10) | copy-start | bytes 6148
  32.6 15.1 %copy-start.3 = (s32[1,8192]{1,0:T(1,128)S(1)}, s32[1,8192]{1,0:T(1,128)}, u32[]{:S(2)}) copy-start(s32[1,8192]{1,0:T(1,128)} %param.15) | copy-start | bytes 98308
  32.6 15.1 %copy-start.4 = (f32[1,8192]{1,0:T(1,128)S(1)}, f32[1,8192]{1,0:T(1,128)}, u32[]{:S(2)}) copy-start(f32[1,8192]{1,0:T(1,128)} %param.12) | copy-start | bytes 98308
  32.6 15.1 %copy-start.5 = (f32[2,32,128]{2,1,0:T(8,128)S(1)}, f32[2,32,128]{2,1,0:T(8,128)}, u32[]{:S(2)}) copy-start(f32[2,32,128]{2,1,0:T(8,128)} %constant.10.clone.phase_ref) | copy-start | bytes 98308
  35.0 12.7 %copy-start = (s32[2,1,8192]{2,1,0:T(1,128)S(1)}, s32[2,1,8192]{2,1,0:T(1,128)}, u32[]{:S(2)}) copy-start(s32[2,1,8192]{2,1,0:T(1,128)} %param.16) | copy-start | bytes 196612
  35.0 12.7 %copy-start.1 = (f32[2,1,8192]{2,1,0:T(1,128)S(1)}, f32[2,1,8192]{2,1,0:T(1,128)}, u32[]{:S(2)}) copy-start(f32[2,1,8192]{2,1,0:T(1,128)} %param.11) | copy-start | bytes 196612
  35.0 12.7 %all-to-all-start.1 = ((f32[8,16,128]{2,1,0:T(8,128)}), f32[8,16,128]{2,1,0:T(8,128)S(1)}, u32[]{:S(2)}, u32[]{:S(2)}) async-start(f32[8,16,128]{2,1,0:T(8,128)} %bitcast.24), calls=%async_computation.1 | async-start | bytes 131072 | tf_op jit(solution)/shard_map/images/all_to_all | solution.py:247
  42.8 4.9 %copy-start.2 = (s32[1,8192]{1,0:T(1,128)S(1)}, s32[1,8192]{1,0:T(1,128)}, u32[]{:S(2)}) copy-start(s32[1,8192]{1,0:T(1,128)} %param.14) | copy-start | bytes 98308
  66.8 19.4 %all-to-all-start.3 = ((f32[64,8,128]{2,1,0:T(8,128)}), f32[64,8,128]{2,1,0:T(8,128)S(1)}, u32[]{:S(2)}, u32[]{:S(2)}) async-start(f32[64,8,128]{2,1,0:T(8,128)} %bitcast.23), calls=%async_computation.3 | async-start | bytes 524288 | tf_op jit(solution)/shard_map/owners/all_to_all | solution.py:261

commit v3 on v2

--- a/solution.py
+++ b/solution.py
@@ -15,7 +15,6 @@
 CHANS = 8
 WITHIN = 4
 CHUNK = 512
-UNROLL = 4
 
 F32 = jnp.float32
 BF16 = jnp.bfloat16
@@ -35,25 +34,10 @@
 
 
 def visibility_kernel(
-    image_ref, taps_ref, phase_ref, slot_ref, plane_ref, offset_ref, data_ref, weight_ref,
-    residual_ref, dirty_ref, grid_ref, total_ref, table_ref,
+    image_ref, table_ref, phase_ref, slot_ref, plane_ref, offset_ref, data_ref, weight_ref,
+    residual_ref, dirty_ref, grid_ref,
 ):
     rows = slot_ref.shape[0]
-    scale = 1.0 / math.sqrt(SIDE)
-    cos_s = phase_ref[0][:, :8] * scale
-    sin_s = phase_ref[1][:, :8] * scale
-
-    def tapped(table, taps):
-        return lax.dot_general(
-            table, taps, (((1,), (1,)), ((), ())),
-            precision=lax.Precision.HIGHEST, preferred_element_type=F32,
-        )
-
-    k_re = tapped(cos_s, taps_ref[0]) - tapped(sin_s, taps_ref[1])
-    k_im = tapped(cos_s, taps_ref[1]) + tapped(sin_s, taps_ref[0])
-    table_ref[0] = jnp.concatenate([k_re] * 4, axis=1)
-    table_ref[1] = jnp.concatenate([k_im] * 4, axis=1)
-
     for low in range(4):
         tiles = [image_ref[pl.ds(high * 4 + low, 8, stride=SLOTS), :] for high in range(4)]
         for step in range(4):
@@ -66,7 +50,6 @@
         [jnp.concatenate([t_high, t_high], axis=1), jnp.concatenate([t_low, t_low], axis=1)],
         axis=0,
     )
-    total_ref[...] = jnp.zeros_like(total_ref)
 
     def spread(x, masks):
         high, low = split(x)
@@ -134,21 +117,15 @@
                 x, y, (((1,), (1,)), ((), ())), preferred_element_type=F32
             )
 
-        return crossed(a_re, jnp.concatenate(z_re_all, axis=1)) + crossed(
-            a_im, jnp.concatenate(z_im_all, axis=1)
-        )
-
-    def step(i, _):
-        part = None
-        for k in range(UNROLL):
-            more = one_chunk((i * UNROLL + k) * per_chunk)
-            part = more if part is None else part + more
-        total_ref[...] += part
-        return 0
-
-    lax.fori_loop(0, rows // (per_chunk * UNROLL), step, 0)
-
-    total = total_ref[...]
+        return crossed(jnp.concatenate(z_re_all, axis=1), a_re) + crossed(
+            jnp.concatenate(z_im_all, axis=1), a_im
+        )
+
+    total = None
+    for first in range(0, rows, per_chunk):
+        more = one_chunk(first)
+        total = more if total is None else total + more
+    total = total.T
     total = total[:, : 4 * SIDE] + total[:, 4 * SIDE :]
     grid_ref[...] = total[: 4 * SIDE] + total[4 * SIDE :]
     for low in range(4):
@@ -159,7 +136,7 @@
             )
 
 
-def visibilities(image, kernels, slot, plane, offset, data, weight):
+def visibilities(image, table, slot, plane, offset, data, weight):
     rows = slot.shape[0]
     return pl.pallas_call(
         visibility_kernel,
@@ -171,19 +148,26 @@
         out_specs=(pl.BlockSpec(memory_space=pltpu.VMEM),) * 2,
         scratch_shapes=[
             pltpu.VMEM((LANES, LANES), F32),
-            pltpu.VMEM((2 * LANES, 2 * LANES), F32),
-            pltpu.VMEM((2, SIDE, LANES), F32),
         ],
-        compiler_params=pltpu.CompilerParams(vmem_limit_bytes=32 * 1024 * 1024),
+        compiler_params=pltpu.CompilerParams(vmem_limit_bytes=24 * 1024 * 1024),
         name="visibilities",
-    )(image, kernels, jnp.asarray(phase_tables()), slot, plane, offset, data, weight)
-
-
-def frequency(channel):
-    return (channel.astype(F32) - 0.5 * (CHANS - 1)) / CHANS
-
-
-def select_kernel(list_ref, model_ref, image_ref):
+    )(image, table, jnp.asarray(phase_tables()), slot, plane, offset, data, weight)
+
+
+def select_kernel(list_ref, model_ref, taps_ref, phase_ref, image_ref, table_ref):
+    scale = 1.0 / math.sqrt(SIDE)
+    cos_s = phase_ref[0] * scale
+    sin_s = phase_ref[1] * scale
+
+    def tapped(table, taps):
+        return jnp.dot(
+            table, taps, precision=lax.Precision.HIGHEST, preferred_element_type=F32
+        )
+
+    k_re = tapped(cos_s, taps_ref[0]) - tapped(sin_s, taps_ref[1])
+    k_im = tapped(cos_s, taps_ref[1]) + tapped(sin_s, taps_ref[0])
+    table_ref[0] = jnp.concatenate([k_re] * 4, axis=1)
+    table_ref[1] = jnp.concatenate([k_im] * 4, axis=1)
     for channel in range(CHANS):
         offset = (channel - 0.5 * (CHANS - 1)) / CHANS
         for slot in range(SLOTS):
@@ -194,17 +178,21 @@
             ] + offset * model_ref[pl.ds(first + WITHIN, 1), :]
 
 
-def select(listed, model):
+def select(listed, model, taps):
     return pl.pallas_call(
         select_kernel,
-        out_shape=jax.ShapeDtypeStruct((CHANS * SLOTS, LANES), F32),
+        out_shape=(
+            jax.ShapeDtypeStruct((CHANS * SLOTS, LANES), F32),
+            jax.ShapeDtypeStruct((2, SIDE, LANES), F32),
+        ),
         in_specs=[
             pl.BlockSpec(memory_space=pltpu.SMEM),
-            pl.BlockSpec(memory_space=pltpu.VMEM),
+            *[pl.BlockSpec(memory_space=pltpu.VMEM)] * 3,
         ],
-        out_specs=pl.BlockSpec(memory_space=pltpu.VMEM),
+        out_specs=(pl.BlockSpec(memory_space=pltpu.VMEM),) * 2,
+        compiler_params=pltpu.CompilerParams(vmem_limit_bytes=8 * 1024 * 1024),
         name="select",
-    )(listed, model)
+    )(listed, model, taps, jnp.asarray(phase_tables()[:, :, :8]))
 
 
 def collect_kernel(list_ref, dirty_ref, owned_ref):
@@ -228,8 +216,27 @@
             pl.BlockSpec(memory_space=pltpu.VMEM),
         ],
         out_specs=pl.BlockSpec(memory_space=pltpu.VMEM),
+        compiler_params=pltpu.CompilerParams(vmem_limit_bytes=8 * 1024 * 1024),
         name="collect",
     )(listed, dirty)
+
+
+def finish_kernel(parts_ref, step_ref):
+    offsets = (np.arange(CHANS) - 0.5 * (CHANS - 1)) / CHANS
+    total = jnp.sum(parts_ref[...], axis=0)
+    step_ref[0] = total[:WITHIN] * (1.0 / CHANS)
+    step_ref[1] = total[WITHIN:] * float(1.0 / np.sum(offsets * offsets))
+
+
+def finish(parts):
+    return pl.pallas_call(
+        finish_kernel,
+        out_shape=jax.ShapeDtypeStruct((2, WITHIN, LANES), F32),
+        in_specs=[pl.BlockSpec(memory_space=pltpu.VMEM)],
+        out_specs=pl.BlockSpec(memory_space=pltpu.VMEM),
+        compiler_params=pltpu.CompilerParams(vmem_limit_bytes=8 * 1024 * 1024),
+        name="finish",
+    )(parts)
 
 
 def shards(model, kernels, vis_data, vis_weight, tile_list, vis_slot, vis_wplane, vis_offset):
@@ -242,12 +249,14 @@
         every = lax.all_to_all(
             jnp.broadcast_to(own, (OWNERS, 2 * WITHIN, LANES)), "vis", 0, 0, tiled=True
         )
-    chosen = select(listed, every.reshape(OWNERS * 2 * WITHIN, LANES))
+    chosen, table = select(
+        listed, every.reshape(OWNERS * 2 * WITHIN, LANES), kernels.transpose(0, 2, 1)
+    )
     with jax.named_scope("images"):
         image = lax.all_to_all(chosen, "chan", 0, 0, tiled=True)
     residual, dirty = visibilities(
         image,
-        kernels,
+        table,
         vis_slot.reshape(rows, LANES),
         vis_wplane.reshape(rows, LANES),
         vis_offset.reshape(2, rows, LANES),
@@ -261,10 +270,7 @@
         summed = lax.all_to_all(
             owned.reshape(OWNERS, 2 * WITHIN, LANES), "vis", 0, 0, tiled=True
         )
-    offsets = (np.arange(CHANS) - 0.5 * (CHANS - 1)) / CHANS
-    term = lax.broadcasted_iota(jnp.int32, (2, WITHIN, LANES), 0)
-    inverse = jnp.where(term == 0, F32(1.0 / CHANS), F32(1.0 / np.sum(offsets * offsets)))
-    model_step = jnp.sum(summed, axis=0).reshape(2, WITHIN, LANES) * inverse
+    model_step = finish(summed)
     return (model_step, residual.reshape(2, 1, count))
 
 

time: 88.5 us -> 81.6 us (0.922)
  blocking collectives: 19.9 us -> 50.2 us
  waiting for transfers between devices: 18.5 us -> 1.29 us
  starting transfers between devices: 32 us -> 17.3 us
  Pallas kernels: 12.8 us -> 9.13 us
    all_to_all x0 -> x2, blocking collectives: none -> 30.9 us  [the longest x1 18.5 us: shards(): lax.all_to_all(owned.reshape(OWNERS, 2 * WITHIN, LANES), 'vis', 0, 0, til...]
    all_to_all x2 -> x0, waiting for transfers between devices: 17.2 us -> none  [the longest x1 12.4 us: shards(): lax.all_to_all(owned.reshape(OWNERS, 2 * WITHIN, LANES), 'vis', 0, 0, til...]
    all_to_all x2 -> x0, starting transfers between devices: 14.8 us -> none  [the longest x1 7.81 us: shards(): image = lax.all_to_all(chosen, 'chan', 0, 0, tiled=True)]
    pallas_call x1, Pallas kernels: 8.11 us -> 5.49 us  [visibilities(): pl.pallas_call(visibility_kernel, out_shape=(jax.ShapeDtypeStruct((2, row...]
    pallas_call x1, Pallas kernels: 2.32 us -> 1.38 us  [collect(): pl.pallas_call(collect_kernel, out_shape=jax.ShapeDtypeStruct((OWNERS * 2...]
    pallas_call x1 -> x2, Pallas kernels: 2.4 us -> 2.25 us  [the longest x1 1.59 us: select(): pl.pallas_call(select_kernel, out_shape=(jax.ShapeDtypeStruct((CHANS * SL...]
  transfers between devices with their start and end apart: 3 -> 1, of which waited for: 3 -> 1; matrix products, arithmetic and copies ran while one was open for 0% -> 0% of each run, Pallas kernels for 0% -> 0%
where the time goes in v3:
time: 81.6 us; the launch traced here: 80 us
  blocking collectives  50.2 us (62%)
  starting transfers between devices  17.3 us (21%)
  Pallas kernels  9.13 us (11%)
  local copies, waits for them, and re-layouts  1.46 us (2%)
  waiting for transfers between devices  1.29 us (2%)
    all_to_all x1, blocking collectives, shards(): lax.all_to_all(owned.reshape(OWNERS, 2 * WITHIN, LANES), 'vis', 0, 0, til...  18.5 us
    all_to_all x1, starting transfers between devices, shards(): lax.all_to_all(jnp.broadcast_to(own, (OWNERS, 2 * WITHIN, LANES)), 'vis',...  17.3 us
    all_to_all x1, blocking collectives, shards(): image = lax.all_to_all(chosen, 'chan', 0, 0, tiled=True)  12.5 us
    all_gather x1, blocking collectives, shards(): lax.all_gather(tile_list.reshape(1, SLOTS), 'chan', axis=0, tiled=True)  11.2 us
    all_to_all x1, blocking collectives, shards(): pieces = lax.all_to_all(dirty, 'chan', 0, 0, tiled=True)  7.98 us
    pallas_call x1, Pallas kernels, visibilities(): pl.pallas_call(visibility_kernel, out_shape=(jax.ShapeDtypeStruct((2, row...  5.49 us
  transfers between devices with their start and end apart: 1, of which 1 were waited for; matrix products, arithmetic and copies ran while one was open for 0% of the time, Pallas kernels for 0%

profile of v3, /device:TPU:1, one launch (start us, length us, event | category | flops | bytes accessed | tf_op | source)
XLA Modules:
  0.0 80.0 jit_solution(14974173338890347363)
XLA Ops:
  0.6 1.4 %broadcast_in_dim.8 = f32[64,8,128]{2,1,0:T(8,128)} broadcast(f32[8,128]{1,0:T(8,128)} %bitcast.29), dimensions={1,2} | broadcast | bytes 266240 | tf_op jit(solution)/shard_map/spread_model/broadcast_in_dim | solution.py:250
  2.0 17.3 %all-to-all-start = ((f32[64,8,128]{2,1,0:T(8,128)}), f32[64,8,128]{2,1,0:T(8,128)S(1)}, u32[]{:S(2)}, u32[]{:S(2)}) async-start(f32[64,8,128]{2,1,0:T(8,128)} %broadcast_in_dim.8), calls=%async_computation | async-start | bytes 524288 | tf_op jit(solution)/shard_map/spread_model/all_to_all | solution.py:249
  19.3 0.0 copy-done.8
  19.3 0.0 copy-start.7
  19.3 11.2 %all-gather = s32[8,1,16]{2,1,0:T(1,128)S(1)} all-gather(s32[1,1,16]{2,1,0:T(1,128)S(1)} %copy-done.8), channel_id=2, replica_groups=mesh['vis'=64,'chan'=8] {'chan'}, dimensions={0}, use_global_device_ids=true | all-gather | bytes 576 | tf_op jit(solution)/shard_map/lists/all_gather | solution.py:246
  30.6 1.3 %all-to-all-done = f32[64,8,128]{2,1,0:T(8,128)S(1)} async-done(((f32[64,8,128]{2,1,0:T(8,128)}), f32[64,8,128]{2,1,0:T(8,128)S(1)}, u32[]{:S(2)}, u32[]{:S(2)}) %all-to-all-start) | async-done | bytes 262176 | tf_op jit(solution)/shard_map/spread_model/all_to_all | solution.py:249
  31.9 0.0 copy-done.2
  31.9 0.0 copy-done.7
  31.9 0.0 copy-start.5
  31.9 0.0 copy-start.6
  31.9 1.6 %select.1 = (f32[128,128]{1,0:T(8,128)S(1)}, f32[2,32,128]{2,1,0:T(8,128)S(1)}) custom-call(s32[8,16]{1,0:T(8,128)S(1)} %bitcast.23, f32[512,128]{1,0:T(8,128)S(1)} %bitcast.15, f32[2,8,32]{2,1,0:T(8,128)S(1)} %bitcast.28, f32[2,32,8]{2,1,0:T(8,128)S(1)} %copy-done.2), custom_call_target="tpu_custom_call" | custom-call | tf_op jit(solution)/shard_map/select/pallas_call | solution.py:182
  33.5 0.0 copy-start
  33.5 0.0 copy-start.1
  33.5 12.5 %all_to_all.32 = f32[8,16,128]{2,1,0:T(8,128)S(1)} all-to-all(f32[8,16,128]{2,1,0:T(8,128)S(1)} %bitcast.20), channel_id=1, replica_groups=mesh['vis'=64,'chan'=8] {'chan'}, dimensions={0} | all-to-all | bytes 131072 | tf_op jit(solution)/shard_map/images/all_to_all | solution.py:256
  46.0 0.0 copy-done.3
  46.0 0.0 copy-done.4
  46.0 0.0 copy-done.5
  46.0 0.0 copy-done.6
  46.0 0.0 copy-done
  46.0 5.5 %visibilities.1 = (f32[2,64,128]{2,1,0:T(8,128)}, f32[128,128]{1,0:T(8,128)S(1)}) custom-call(f32[128,128]{1,0:T(8,128)S(1)} %bitcast.17, f32[2,32,128]{2,1,0:T(8,128)S(1)} %get-tuple-element.7.table_ref, f32[2,32,128]{2,1,0:T(8,128)S(1)} %copy-done.6, s32[64,128]{1,0:T(8,128)S(1)} %bitcast.25, s32[64,128]{1,0:T(8,128)S(1)} %bitcast.26, ...), custom_call_target="tpu_custom_call" | custom-call | tf_op jit(solution)/shard_map/visibilities/pallas_call | solution.py:141
  51.5 8.0 %all_to_all.33 = f32[8,16,128]{2,1,0:T(8,128)S(1)} all-to-all(f32[8,16,128]{2,1,0:T(8,128)S(1)} %bitcast.19), channel_id=1, replica_groups=mesh['vis'=64,'chan'=8] {'chan'}, dimensions={0} | all-to-all | bytes 131072 | tf_op jit(solution)/shard_map/dirty_cells/all_to_all | solution.py:267
  59.5 1.4 %collect.1 = f32[512,128]{1,0:T(8,128)S(1)} custom-call(s32[8,16]{1,0:T(8,128)S(1)} %bitcast.24, f32[128,128]{1,0:T(8,128)S(1)} %bitcast.18), custom_call_target="tpu_custom_call" | custom-call | tf_op jit(solution)/shard_map/collect/pallas_call | solution.py:211
  60.9 18.5 %all_to_all.34.parts_ref = f32[64,8,128]{2,1,0:T(8,128)S(1)} all-to-all(f32[64,8,128]{2,1,0:T(8,128)S(1)} %bitcast.16), channel_id=1, replica_groups=mesh['vis'=64,'chan'=8] {'vis'}, dimensions={0} | all-to-all | bytes 524288 | tf_op jit(solution)/shard_map/owners/all_to_all | solution.py:270
  79.4 0.7 finish.1
  (5 shorter events, 0.0 us)
Async XLA Ops:
  2.0 17.3 %copy-start.8 = (s32[1,1,16]{2,1,0:T(1,128)S(1)}, s32[1,1,16]{2,1,0:T(1,128)}, u32[]{:S(2)}) copy-start(s32[1,1,16]{2,1,0:T(1,128)} %param.14) | copy-start | bytes 196
  2.0 29.8 %copy-start.2 = (f32[2,32,8]{2,1,0:T(8,128)S(1)}, f32[2,32,8]{2,1,0:T(8,128)}, u32[]{:S(2)}) copy-start(f32[2,32,8]{2,1,0:T(8,128)} %constant.4.clone.phase_ref) | copy-start | bytes 6148
  2.0 29.8 %all-to-all-start = ((f32[64,8,128]{2,1,0:T(8,128)}), f32[64,8,128]{2,1,0:T(8,128)S(1)}, u32[]{:S(2)}, u32[]{:S(2)}) async-start(f32[64,8,128]{2,1,0:T(8,128)} %broadcast_in_dim.8), calls=%async_computation | async-start | bytes 524288 | tf_op jit(solution)/shard_map/spread_model/all_to_all | solution.py:249
  19.3 12.5 %copy-start.7 = (f32[2,32,8]{1,2,0:T(8,128)S(1)}, f32[2,32,8]{1,2,0:T(8,128)}, u32[]{:S(2)}) copy-start(f32[2,32,8]{1,2,0:T(8,128)} %param.11) | copy-start | bytes 6148
  31.9 14.1 %copy-start.3 = (s32[1,8192]{1,0:T(1,128)S(1)}, s32[1,8192]{1,0:T(1,128)}, u32[]{:S(2)}) copy-start(s32[1,8192]{1,0:T(1,128)} %param.15) | copy-start | bytes 98308
  31.9 14.1 %copy-start.4 = (s32[1,8192]{1,0:T(1,128)S(1)}, s32[1,8192]{1,0:T(1,128)}, u32[]{:S(2)}) copy-start(s32[1,8192]{1,0:T(1,128)} %param.16) | copy-start | bytes 98308
  31.9 14.1 %copy-start.5 = (f32[1,8192]{1,0:T(1,128)S(1)}, f32[1,8192]{1,0:T(1,128)}, u32[]{:S(2)}) copy-start(f32[1,8192]{1,0:T(1,128)} %param.13) | copy-start | bytes 98308
  31.9 14.1 %copy-start.6 = (f32[2,32,128]{2,1,0:T(8,128)S(1)}, f32[2,32,128]{2,1,0:T(8,128)}, u32[]{:S(2)}) copy-start(f32[2,32,128]{2,1,0:T(8,128)} %constant.5.clone.phase_ref) | copy-start | bytes 98308
  33.5 12.5 %copy-start = (s32[2,1,8192]{2,1,0:T(1,128)S(1)}, s32[2,1,8192]{2,1,0:T(1,128)}, u32[]{:S(2)}) copy-start(s32[2,1,8192]{2,1,0:T(1,128)} %param.17) | copy-start | bytes 196612
  33.5 12.5 %copy-start.1 = (f32[2,1,8192]{2,1,0:T(1,128)S(1)}, f32[2,1,8192]{2,1,0:T(1,128)}, u32[]{:S(2)}) copy-start(f32[2,1,8192]{2,1,0:T(1,128)} %param.12) | copy-start | bytes 196612

commit v4 on v3

--- a/solution.py
+++ b/solution.py
@@ -172,7 +172,7 @@
         offset = (channel - 0.5 * (CHANS - 1)) / CHANS
         for slot in range(SLOTS):
             tile = list_ref[channel, slot]
-            first = (tile // WITHIN) * (2 * WITHIN) + tile % WITHIN
+            first = 2 * tile - (tile & (WITHIN - 1))
             image_ref[pl.ds(channel * SLOTS + slot, 1), :] = model_ref[
                 pl.ds(first, 1), :
             ] + offset * model_ref[pl.ds(first + WITHIN, 1), :]
@@ -199,12 +199,16 @@
     owned_ref[...] = jnp.zeros_like(owned_ref)
     for channel in range(CHANS):
         offset = (channel - 0.5 * (CHANS - 1)) / CHANS
+        firsts = []
         for slot in range(SLOTS):
             tile = list_ref[channel, slot]
-            first = (tile // WITHIN) * (2 * WITHIN) + tile % WITHIN
-            row = dirty_ref[pl.ds(channel * SLOTS + slot, 1), :]
-            owned_ref[pl.ds(first, 1), :] += row
-            owned_ref[pl.ds(first + WITHIN, 1), :] += offset * row
+            firsts.append(2 * tile - (tile & (WITHIN - 1)))
+        rows = [dirty_ref[pl.ds(channel * SLOTS + slot, 1), :] for slot in range(SLOTS)]
+        zeros = [owned_ref[pl.ds(first, 1), :] for first in firsts]
+        ones = [owned_ref[pl.ds(first + WITHIN, 1), :] for first in firsts]
+        for first, row, zero, one in zip(firsts, rows, zeros, ones):
+            owned_ref[pl.ds(first, 1), :] = zero + row
+            owned_ref[pl.ds(first + WITHIN, 1), :] = one + offset * row
 
 
 def collect(listed, dirty):

time: 81.6 us -> 80.4 us (0.985)
  Pallas kernels: 9.13 us -> 7.95 us
where the time goes in v4:
time: 80.4 us; the launch traced here: 78.9 us
  blocking collectives  50.2 us (62%)
  starting transfers between devices  17.3 us (22%)
  Pallas kernels  7.95 us (10%)
  local copies, waits for them, and re-layouts  1.46 us (2%)
  waiting for transfers between devices  1.29 us (2%)
    all_to_all x1, blocking collectives, shards(): lax.all_to_all(owned.reshape(OWNERS, 2 * WITHIN, LANES), 'vis', 0, 0, til...  18.5 us
    all_to_all x1, starting transfers between devices, shards(): lax.all_to_all(jnp.broadcast_to(own, (OWNERS, 2 * WITHIN, LANES)), 'vis',...  17.3 us
    all_to_all x1, blocking collectives, shards(): image = lax.all_to_all(chosen, 'chan', 0, 0, tiled=True)  12.5 us
    all_gather x1, blocking collectives, shards(): lax.all_gather(tile_list.reshape(1, SLOTS), 'chan', axis=0, tiled=True)  11.2 us
    all_to_all x1, blocking collectives, shards(): pieces = lax.all_to_all(dirty, 'chan', 0, 0, tiled=True)  7.98 us
    pallas_call x1, Pallas kernels, visibilities(): pl.pallas_call(visibility_kernel, out_shape=(jax.ShapeDtypeStruct((2, row...  5.49 us
  transfers between devices with their start and end apart: 1, of which 1 were waited for; matrix products, arithmetic and copies ran while one was open for 0% of the time, Pallas kernels for 0%

profile of v4, /device:TPU:1, one launch (start us, length us, event | category | flops | bytes accessed | tf_op | source)
XLA Modules:
  0.0 78.9 jit_solution(17800093639115961699)
XLA Ops:
  0.6 1.4 %broadcast_in_dim.8 = f32[64,8,128]{2,1,0:T(8,128)} broadcast(f32[8,128]{1,0:T(8,128)} %bitcast.29), dimensions={1,2} | broadcast | bytes 266240 | tf_op jit(solution)/shard_map/spread_model/broadcast_in_dim | solution.py:254
  2.0 17.3 %all-to-all-start = ((f32[64,8,128]{2,1,0:T(8,128)}), f32[64,8,128]{2,1,0:T(8,128)S(1)}, u32[]{:S(2)}, u32[]{:S(2)}) async-start(f32[64,8,128]{2,1,0:T(8,128)} %broadcast_in_dim.8), calls=%async_computation | async-start | bytes 524288 | tf_op jit(solution)/shard_map/spread_model/all_to_all | solution.py:253
  19.3 0.0 copy-done.8
  19.3 0.0 copy-start.7
  19.3 11.2 %all-gather = s32[8,1,16]{2,1,0:T(1,128)S(1)} all-gather(s32[1,1,16]{2,1,0:T(1,128)S(1)} %copy-done.8), channel_id=2, replica_groups=mesh['vis'=64,'chan'=8] {'chan'}, dimensions={0}, use_global_device_ids=true | all-gather | bytes 576 | tf_op jit(solution)/shard_map/lists/all_gather | solution.py:250
  30.6 1.3 %all-to-all-done = f32[64,8,128]{2,1,0:T(8,128)S(1)} async-done(((f32[64,8,128]{2,1,0:T(8,128)}), f32[64,8,128]{2,1,0:T(8,128)S(1)}, u32[]{:S(2)}, u32[]{:S(2)}) %all-to-all-start) | async-done | bytes 262176 | tf_op jit(solution)/shard_map/spread_model/all_to_all | solution.py:253
  31.9 0.0 copy-done.2
  31.9 0.0 copy-done.7
  31.9 0.0 copy-start.5
  31.9 0.0 copy-start.6
  31.9 1.0 %select.1 = (f32[128,128]{1,0:T(8,128)S(1)}, f32[2,32,128]{2,1,0:T(8,128)S(1)}) custom-call(s32[8,16]{1,0:T(8,128)S(1)} %bitcast.23, f32[512,128]{1,0:T(8,128)S(1)} %bitcast.15, f32[2,8,32]{2,1,0:T(8,128)S(1)} %bitcast.28, f32[2,32,8]{2,1,0:T(8,128)S(1)} %copy-done.2), custom_call_target="tpu_custom_call" | custom-call | tf_op jit(solution)/shard_map/select/pallas_call | solution.py:182
  32.9 0.0 copy-start
  32.9 0.0 copy-start.1
  32.9 12.5 %all_to_all.32 = f32[8,16,128]{2,1,0:T(8,128)S(1)} all-to-all(f32[8,16,128]{2,1,0:T(8,128)S(1)} %bitcast.20), channel_id=1, replica_groups=mesh['vis'=64,'chan'=8] {'chan'}, dimensions={0} | all-to-all | bytes 131072 | tf_op jit(solution)/shard_map/images/all_to_all | solution.py:260
  45.4 0.0 copy-done.3
  45.4 0.0 copy-done.4
  45.4 0.0 copy-done.5
  45.4 0.0 copy-done.6
  45.4 0.0 copy-done
  45.4 5.5 %visibilities.1 = (f32[2,64,128]{2,1,0:T(8,128)}, f32[128,128]{1,0:T(8,128)S(1)}) custom-call(f32[128,128]{1,0:T(8,128)S(1)} %bitcast.17, f32[2,32,128]{2,1,0:T(8,128)S(1)} %get-tuple-element.7.table_ref, f32[2,32,128]{2,1,0:T(8,128)S(1)} %copy-done.6, s32[64,128]{1,0:T(8,128)S(1)} %bitcast.25, s32[64,128]{1,0:T(8,128)S(1)} %bitcast.26, ...), custom_call_target="tpu_custom_call" | custom-call | tf_op jit(solution)/shard_map/visibilities/pallas_call | solution.py:141
  50.9 8.0 %all_to_all.33 = f32[8,16,128]{2,1,0:T(8,128)S(1)} all-to-all(f32[8,16,128]{2,1,0:T(8,128)S(1)} %bitcast.19), channel_id=1, replica_groups=mesh['vis'=64,'chan'=8] {'chan'}, dimensions={0} | all-to-all | bytes 131072 | tf_op jit(solution)/shard_map/dirty_cells/all_to_all | solution.py:271
  58.9 0.8 %collect.1 = f32[512,128]{1,0:T(8,128)S(1)} custom-call(s32[8,16]{1,0:T(8,128)S(1)} %bitcast.24, f32[128,128]{1,0:T(8,128)S(1)} %bitcast.18), custom_call_target="tpu_custom_call" | custom-call | tf_op jit(solution)/shard_map/collect/pallas_call | solution.py:215
  59.7 18.5 %all_to_all.34.parts_ref = f32[64,8,128]{2,1,0:T(8,128)S(1)} all-to-all(f32[64,8,128]{2,1,0:T(8,128)S(1)} %bitcast.16), channel_id=1, replica_groups=mesh['vis'=64,'chan'=8] {'vis'}, dimensions={0} | all-to-all | bytes 524288 | tf_op jit(solution)/shard_map/owners/all_to_all | solution.py:274
  78.2 0.7 finish.1
  (5 shorter events, 0.0 us)
Async XLA Ops:
  2.0 17.3 %copy-start.8 = (s32[1,1,16]{2,1,0:T(1,128)S(1)}, s32[1,1,16]{2,1,0:T(1,128)}, u32[]{:S(2)}) copy-start(s32[1,1,16]{2,1,0:T(1,128)} %param.14) | copy-start | bytes 196
  2.0 29.8 %copy-start.2 = (f32[2,32,8]{2,1,0:T(8,128)S(1)}, f32[2,32,8]{2,1,0:T(8,128)}, u32[]{:S(2)}) copy-start(f32[2,32,8]{2,1,0:T(8,128)} %constant.4.clone.phase_ref) | copy-start | bytes 6148
  2.0 29.8 %all-to-all-start = ((f32[64,8,128]{2,1,0:T(8,128)}), f32[64,8,128]{2,1,0:T(8,128)S(1)}, u32[]{:S(2)}, u32[]{:S(2)}) async-start(f32[64,8,128]{2,1,0:T(8,128)} %broadcast_in_dim.8), calls=%async_computation | async-start | bytes 524288 | tf_op jit(solution)/shard_map/spread_model/all_to_all | solution.py:253
  19.3 12.5 %copy-start.7 = (f32[2,32,8]{1,2,0:T(8,128)S(1)}, f32[2,32,8]{1,2,0:T(8,128)}, u32[]{:S(2)}) copy-start(f32[2,32,8]{1,2,0:T(8,128)} %param.11) | copy-start | bytes 6148
  31.9 13.5 %copy-start.3 = (s32[1,8192]{1,0:T(1,128)S(1)}, s32[1,8192]{1,0:T(1,128)}, u32[]{:S(2)}) copy-start(s32[1,8192]{1,0:T(1,128)} %param.15) | copy-start | bytes 98308
  31.9 13.5 %copy-start.4 = (s32[1,8192]{1,0:T(1,128)S(1)}, s32[1,8192]{1,0:T(1,128)}, u32[]{:S(2)}) copy-start(s32[1,8192]{1,0:T(1,128)} %param.16) | copy-start | bytes 98308
  31.9 13.5 %copy-start.5 = (f32[1,8192]{1,0:T(1,128)S(1)}, f32[1,8192]{1,0:T(1,128)}, u32[]{:S(2)}) copy-start(f32[1,8192]{1,0:T(1,128)} %param.13) | copy-start | bytes 98308
  31.9 13.5 %copy-start.6 = (f32[2,32,128]{2,1,0:T(8,128)S(1)}, f32[2,32,128]{2,1,0:T(8,128)}, u32[]{:S(2)}) copy-start(f32[2,32,128]{2,1,0:T(8,128)} %constant.5.clone.phase_ref) | copy-start | bytes 98308
  32.9 12.5 %copy-start = (s32[2,1,8192]{2,1,0:T(1,128)S(1)}, s32[2,1,8192]{2,1,0:T(1,128)}, u32[]{:S(2)}) copy-start(s32[2,1,8192]{2,1,0:T(1,128)} %param.17) | copy-start | bytes 196612
  32.9 12.5 %copy-start.1 = (f32[2,1,8192]{2,1,0:T(1,128)S(1)}, f32[2,1,8192]{2,1,0:T(1,128)}, u32[]{:S(2)}) copy-start(f32[2,1,8192]{2,1,0:T(1,128)} %param.12) | copy-start | bytes 196612

commit v5 on v4

--- a/solution.py
+++ b/solution.py
@@ -125,9 +125,8 @@
     for first in range(0, rows, per_chunk):
         more = one_chunk(first)
         total = more if total is None else total + more
-    total = total.T
     total = total[:, : 4 * SIDE] + total[:, 4 * SIDE :]
-    grid_ref[...] = total[: 4 * SIDE] + total[4 * SIDE :]
+    grid_ref[...] = (total[: 4 * SIDE] + total[4 * SIDE :]).T
     for low in range(4):
         parts = [grid_ref[pl.ds(low * SIDE + s, 8, stride=4), :] for s in range(4)]
         for high in range(4):

time: 80.4 us -> 80.4 us (level)
  no operation moved by 1% of the time
where the time goes in v5:
time: 80.4 us; the launch traced here: 78.9 us
  blocking collectives  50.2 us (62%)
  starting transfers between devices  17.3 us (22%)
  Pallas kernels  7.95 us (10%)
  local copies, waits for them, and re-layouts  1.46 us (2%)
  waiting for transfers between devices  1.29 us (2%)
    all_to_all x1, blocking collectives, shards(): lax.all_to_all(owned.reshape(OWNERS, 2 * WITHIN, LANES), 'vis', 0, 0, til...  18.5 us
    all_to_all x1, starting transfers between devices, shards(): lax.all_to_all(jnp.broadcast_to(own, (OWNERS, 2 * WITHIN, LANES)), 'vis',...  17.3 us
    all_to_all x1, blocking collectives, shards(): image = lax.all_to_all(chosen, 'chan', 0, 0, tiled=True)  12.5 us
    all_gather x1, blocking collectives, shards(): lax.all_gather(tile_list.reshape(1, SLOTS), 'chan', axis=0, tiled=True)  11.2 us
    all_to_all x1, blocking collectives, shards(): pieces = lax.all_to_all(dirty, 'chan', 0, 0, tiled=True)  7.98 us
    pallas_call x1, Pallas kernels, visibilities(): pl.pallas_call(visibility_kernel, out_shape=(jax.ShapeDtypeStruct((2, row...  5.49 us
  transfers between devices with their start and end apart: 1, of which 1 were waited for; matrix products, arithmetic and copies ran while one was open for 0% of the time, Pallas kernels for 0%

profile of v5, /device:TPU:1, one launch (start us, length us, event | category | flops | bytes accessed | tf_op | source)
XLA Modules:
  0.0 78.9 jit_solution(5770487398772877087)
XLA Ops:
  0.6 1.4 %broadcast_in_dim.8 = f32[64,8,128]{2,1,0:T(8,128)} broadcast(f32[8,128]{1,0:T(8,128)} %bitcast.29), dimensions={1,2} | broadcast | bytes 266240 | tf_op jit(solution)/shard_map/spread_model/broadcast_in_dim | solution.py:253
  2.0 17.3 %all-to-all-start = ((f32[64,8,128]{2,1,0:T(8,128)}), f32[64,8,128]{2,1,0:T(8,128)S(1)}, u32[]{:S(2)}, u32[]{:S(2)}) async-start(f32[64,8,128]{2,1,0:T(8,128)} %broadcast_in_dim.8), calls=%async_computation | async-start | bytes 524288 | tf_op jit(solution)/shard_map/spread_model/all_to_all | solution.py:252
  19.3 0.0 copy-done.8
  19.3 0.0 copy-start.7
  19.3 11.2 %all-gather = s32[8,1,16]{2,1,0:T(1,128)S(1)} all-gather(s32[1,1,16]{2,1,0:T(1,128)S(1)} %copy-done.8), channel_id=2, replica_groups=mesh['vis'=64,'chan'=8] {'chan'}, dimensions={0}, use_global_device_ids=true | all-gather | bytes 576 | tf_op jit(solution)/shard_map/lists/all_gather | solution.py:249
  30.6 1.3 %all-to-all-done = f32[64,8,128]{2,1,0:T(8,128)S(1)} async-done(((f32[64,8,128]{2,1,0:T(8,128)}), f32[64,8,128]{2,1,0:T(8,128)S(1)}, u32[]{:S(2)}, u32[]{:S(2)}) %all-to-all-start) | async-done | bytes 262176 | tf_op jit(solution)/shard_map/spread_model/all_to_all | solution.py:252
  31.9 0.0 copy-done.2
  31.9 0.0 copy-done.7
  31.9 0.0 copy-start.5
  31.9 0.0 copy-start.6
  31.9 1.0 %select.1 = (f32[128,128]{1,0:T(8,128)S(1)}, f32[2,32,128]{2,1,0:T(8,128)S(1)}) custom-call(s32[8,16]{1,0:T(8,128)S(1)} %bitcast.23, f32[512,128]{1,0:T(8,128)S(1)} %bitcast.15, f32[2,8,32]{2,1,0:T(8,128)S(1)} %bitcast.28, f32[2,32,8]{2,1,0:T(8,128)S(1)} %copy-done.2), custom_call_target="tpu_custom_call" | custom-call | tf_op jit(solution)/shard_map/select/pallas_call | solution.py:181
  32.9 0.0 copy-start
  32.9 0.0 copy-start.1
  32.9 12.5 %all_to_all.32 = f32[8,16,128]{2,1,0:T(8,128)S(1)} all-to-all(f32[8,16,128]{2,1,0:T(8,128)S(1)} %bitcast.20), channel_id=1, replica_groups=mesh['vis'=64,'chan'=8] {'chan'}, dimensions={0} | all-to-all | bytes 131072 | tf_op jit(solution)/shard_map/images/all_to_all | solution.py:259
  45.4 0.0 copy-done.3
  45.4 0.0 copy-done.4
  45.4 0.0 copy-done.5
  45.4 0.0 copy-done.6
  45.4 0.0 copy-done
  45.4 5.5 %visibilities.1 = (f32[2,64,128]{2,1,0:T(8,128)}, f32[128,128]{1,0:T(8,128)S(1)}) custom-call(f32[128,128]{1,0:T(8,128)S(1)} %bitcast.17, f32[2,32,128]{2,1,0:T(8,128)S(1)} %get-tuple-element.7.table_ref, f32[2,32,128]{2,1,0:T(8,128)S(1)} %copy-done.6, s32[64,128]{1,0:T(8,128)S(1)} %bitcast.25, s32[64,128]{1,0:T(8,128)S(1)} %bitcast.26, ...), custom_call_target="tpu_custom_call" | custom-call | tf_op jit(solution)/shard_map/visibilities/pallas_call | solution.py:140
  50.9 8.0 %all_to_all.33 = f32[8,16,128]{2,1,0:T(8,128)S(1)} all-to-all(f32[8,16,128]{2,1,0:T(8,128)S(1)} %bitcast.19), channel_id=1, replica_groups=mesh['vis'=64,'chan'=8] {'chan'}, dimensions={0} | all-to-all | bytes 131072 | tf_op jit(solution)/shard_map/dirty_cells/all_to_all | solution.py:270
  58.9 0.8 %collect.1 = f32[512,128]{1,0:T(8,128)S(1)} custom-call(s32[8,16]{1,0:T(8,128)S(1)} %bitcast.24, f32[128,128]{1,0:T(8,128)S(1)} %bitcast.18), custom_call_target="tpu_custom_call" | custom-call | tf_op jit(solution)/shard_map/collect/pallas_call | solution.py:214
  59.7 18.5 %all_to_all.34.parts_ref = f32[64,8,128]{2,1,0:T(8,128)S(1)} all-to-all(f32[64,8,128]{2,1,0:T(8,128)S(1)} %bitcast.16), channel_id=1, replica_groups=mesh['vis'=64,'chan'=8] {'vis'}, dimensions={0} | all-to-all | bytes 524288 | tf_op jit(solution)/shard_map/owners/all_to_all | solution.py:273
  78.2 0.7 finish.1
  (5 shorter events, 0.0 us)
Async XLA Ops:
  2.0 17.3 %copy-start.8 = (s32[1,1,16]{2,1,0:T(1,128)S(1)}, s32[1,1,16]{2,1,0:T(1,128)}, u32[]{:S(2)}) copy-start(s32[1,1,16]{2,1,0:T(1,128)} %param.14) | copy-start | bytes 196
  2.0 29.8 %copy-start.2 = (f32[2,32,8]{2,1,0:T(8,128)S(1)}, f32[2,32,8]{2,1,0:T(8,128)}, u32[]{:S(2)}) copy-start(f32[2,32,8]{2,1,0:T(8,128)} %constant.4.clone.phase_ref) | copy-start | bytes 6148
  2.0 29.8 %all-to-all-start = ((f32[64,8,128]{2,1,0:T(8,128)}), f32[64,8,128]{2,1,0:T(8,128)S(1)}, u32[]{:S(2)}, u32[]{:S(2)}) async-start(f32[64,8,128]{2,1,0:T(8,128)} %broadcast_in_dim.8), calls=%async_computation | async-start | bytes 524288 | tf_op jit(solution)/shard_map/spread_model/all_to_all | solution.py:252
  19.3 12.5 %copy-start.7 = (f32[2,32,8]{1,2,0:T(8,128)S(1)}, f32[2,32,8]{1,2,0:T(8,128)}, u32[]{:S(2)}) copy-start(f32[2,32,8]{1,2,0:T(8,128)} %param.11) | copy-start | bytes 6148
  31.9 13.5 %copy-start.3 = (s32[1,8192]{1,0:T(1,128)S(1)}, s32[1,8192]{1,0:T(1,128)}, u32[]{:S(2)}) copy-start(s32[1,8192]{1,0:T(1,128)} %param.15) | copy-start | bytes 98308
  31.9 13.5 %copy-start.4 = (s32[1,8192]{1,0:T(1,128)S(1)}, s32[1,8192]{1,0:T(1,128)}, u32[]{:S(2)}) copy-start(s32[1,8192]{1,0:T(1,128)} %param.16) | copy-start | bytes 98308
  31.9 13.5 %copy-start.5 = (f32[1,8192]{1,0:T(1,128)S(1)}, f32[1,8192]{1,0:T(1,128)}, u32[]{:S(2)}) copy-start(f32[1,8192]{1,0:T(1,128)} %param.13) | copy-start | bytes 98308
  31.9 13.5 %copy-start.6 = (f32[2,32,128]{2,1,0:T(8,128)S(1)}, f32[2,32,128]{2,1,0:T(8,128)}, u32[]{:S(2)}) copy-start(f32[2,32,128]{2,1,0:T(8,128)} %constant.5.clone.phase_ref) | copy-start | bytes 98308
  32.9 12.5 %copy-start = (s32[2,1,8192]{2,1,0:T(1,128)S(1)}, s32[2,1,8192]{2,1,0:T(1,128)}, u32[]{:S(2)}) copy-start(s32[2,1,8192]{2,1,0:T(1,128)} %param.17) | copy-start | bytes 196612
  32.9 12.5 %copy-start.1 = (f32[2,1,8192]{2,1,0:T(1,128)S(1)}, f32[2,1,8192]{2,1,0:T(1,128)}, u32[]{:S(2)}) copy-start(f32[2,1,8192]{2,1,0:T(1,128)} %param.12) | copy-start | bytes 196612

commit v6 on v5

--- a/solution.py
+++ b/solution.py
@@ -154,17 +154,11 @@
 
 
 def select_kernel(list_ref, model_ref, taps_ref, phase_ref, image_ref, table_ref):
-    scale = 1.0 / math.sqrt(SIDE)
-    cos_s = phase_ref[0] * scale
-    sin_s = phase_ref[1] * scale
-
-    def tapped(table, taps):
-        return jnp.dot(
-            table, taps, precision=lax.Precision.HIGHEST, preferred_element_type=F32
-        )
-
-    k_re = tapped(cos_s, taps_ref[0]) - tapped(sin_s, taps_ref[1])
-    k_im = tapped(cos_s, taps_ref[1]) + tapped(sin_s, taps_ref[0])
+    table = jnp.dot(
+        phase_ref[...], taps_ref[...],
+        precision=lax.Precision.HIGHEST, preferred_element_type=F32,
+    )
+    k_re, k_im = table[:SIDE], table[SIDE:]
     table_ref[0] = jnp.concatenate([k_re] * 4, axis=1)
     table_ref[1] = jnp.concatenate([k_im] * 4, axis=1)
     for channel in range(CHANS):
@@ -178,6 +172,8 @@
 
 
 def select(listed, model, taps):
+    cosine, sine = phase_tables()[:, :, :8] / math.sqrt(SIDE)
+    turned = np.block([[cosine, -sine], [sine, cosine]]).astype(np.float32)
     return pl.pallas_call(
         select_kernel,
         out_shape=(
@@ -191,7 +187,7 @@
         out_specs=(pl.BlockSpec(memory_space=pltpu.VMEM),) * 2,
         compiler_params=pltpu.CompilerParams(vmem_limit_bytes=8 * 1024 * 1024),
         name="select",
-    )(listed, model, taps, jnp.asarray(phase_tables()[:, :, :8]))
+    )(listed, model, taps, jnp.asarray(turned))
 
 
 def collect_kernel(list_ref, dirty_ref, owned_ref):
@@ -253,7 +249,7 @@
             jnp.broadcast_to(own, (OWNERS, 2 * WITHIN, LANES)), "vis", 0, 0, tiled=True
         )
     chosen, table = select(
-        listed, every.reshape(OWNERS * 2 * WITHIN, LANES), kernels.transpose(0, 2, 1)
+        listed, every.reshape(OWNERS * 2 * WITHIN, LANES), kernels.transpose(0, 2, 1).reshape(16, SIDE)
     )
     with jax.named_scope("images"):
         image = lax.all_to_all(chosen, "chan", 0, 0, tiled=True)

time: 80.4 us -> 80.3 us (level)
  no operation moved by 1% of the time
where the time goes in v6:
time: 80.3 us; the launch traced here: 78.8 us
  blocking collectives  50.2 us (63%)
  starting transfers between devices  17.3 us (22%)
  Pallas kernels  7.88 us (10%)
  local copies, waits for them, and re-layouts  1.46 us (2%)
  waiting for transfers between devices  1.29 us (2%)
    all_to_all x1, blocking collectives, shards(): lax.all_to_all(owned.reshape(OWNERS, 2 * WITHIN, LANES), 'vis', 0, 0, til...  18.5 us
    all_to_all x1, starting transfers between devices, shards(): lax.all_to_all(jnp.broadcast_to(own, (OWNERS, 2 * WITHIN, LANES)), 'vis',...  17.3 us
    all_to_all x1, blocking collectives, shards(): image = lax.all_to_all(chosen, 'chan', 0, 0, tiled=True)  12.5 us
    all_gather x1, blocking collectives, shards(): lax.all_gather(tile_list.reshape(1, SLOTS), 'chan', axis=0, tiled=True)  11.2 us
    all_to_all x1, blocking collectives, shards(): pieces = lax.all_to_all(dirty, 'chan', 0, 0, tiled=True)  7.99 us
    pallas_call x1, Pallas kernels, visibilities(): pl.pallas_call(visibility_kernel, out_shape=(jax.ShapeDtypeStruct((2, row...  5.49 us
  transfers between devices with their start and end apart: 1, of which 1 were waited for; matrix products, arithmetic and copies ran while one was open for 0% of the time, Pallas kernels for 0%

profile of v6, /device:TPU:1, one launch (start us, length us, event | category | flops | bytes accessed | tf_op | source)
XLA Modules:
  0.0 78.8 jit_solution(6578083790581006294)
XLA Ops:
  0.6 1.4 %broadcast_in_dim.8 = f32[64,8,128]{2,1,0:T(8,128)} broadcast(f32[8,128]{1,0:T(8,128)} %bitcast.31), dimensions={1,2} | broadcast | bytes 266240 | tf_op jit(solution)/shard_map/spread_model/broadcast_in_dim | solution.py:249
  2.0 17.3 %all-to-all-start = ((f32[64,8,128]{2,1,0:T(8,128)}), f32[64,8,128]{2,1,0:T(8,128)S(1)}, u32[]{:S(2)}, u32[]{:S(2)}) async-start(f32[64,8,128]{2,1,0:T(8,128)} %broadcast_in_dim.8), calls=%async_computation | async-start | bytes 524288 | tf_op jit(solution)/shard_map/spread_model/all_to_all | solution.py:248
  19.3 0.0 copy-done.8
  19.3 0.0 copy-start.7
  19.3 11.2 %all-gather = s32[8,1,16]{2,1,0:T(1,128)S(1)} all-gather(s32[1,1,16]{2,1,0:T(1,128)S(1)} %copy-done.8), channel_id=2, replica_groups=mesh['vis'=64,'chan'=8] {'chan'}, dimensions={0}, use_global_device_ids=true | all-gather | bytes 576 | tf_op jit(solution)/shard_map/lists/all_gather | solution.py:245
  30.6 1.3 %all-to-all-done = f32[64,8,128]{2,1,0:T(8,128)S(1)} async-done(((f32[64,8,128]{2,1,0:T(8,128)}), f32[64,8,128]{2,1,0:T(8,128)S(1)}, u32[]{:S(2)}, u32[]{:S(2)}) %all-to-all-start) | async-done | bytes 262176 | tf_op jit(solution)/shard_map/spread_model/all_to_all | solution.py:248
  31.9 0.0 copy-done.2
  31.9 0.0 copy-done.7
  31.9 0.0 copy-start.5
  31.9 0.0 copy-start.6
  31.9 0.9 %select.1 = (f32[128,128]{1,0:T(8,128)S(1)}, f32[2,32,128]{2,1,0:T(8,128)S(1)}) custom-call(s32[8,16]{1,0:T(8,128)S(1)} %bitcast.25, f32[512,128]{1,0:T(8,128)S(1)} %bitcast.17, f32[16,32]{1,0:T(8,128)S(1)} %bitcast.30, f32[64,16]{1,0:T(8,128)S(1)} %copy-done.2), custom_call_target="tpu_custom_call" | custom-call | tf_op jit(solution)/shard_map/select/pallas_call | solution.py:177
  32.9 0.0 copy-start
  32.9 0.0 copy-start.1
  32.9 12.5 %all_to_all.32 = f32[8,16,128]{2,1,0:T(8,128)S(1)} all-to-all(f32[8,16,128]{2,1,0:T(8,128)S(1)} %bitcast.22), channel_id=1, replica_groups=mesh['vis'=64,'chan'=8] {'chan'}, dimensions={0} | all-to-all | bytes 131072 | tf_op jit(solution)/shard_map/images/all_to_all | solution.py:255
  45.3 0.0 copy-done.3
  45.3 0.0 copy-done.4
  45.3 0.0 copy-done.5
  45.3 0.0 copy-done.6
  45.4 0.0 copy-done
  45.4 5.5 %visibilities.1 = (f32[2,64,128]{2,1,0:T(8,128)}, f32[128,128]{1,0:T(8,128)S(1)}) custom-call(f32[128,128]{1,0:T(8,128)S(1)} %bitcast.19, f32[2,32,128]{2,1,0:T(8,128)S(1)} %get-tuple-element.7.table_ref, f32[2,32,128]{2,1,0:T(8,128)S(1)} %copy-done.6, s32[64,128]{1,0:T(8,128)S(1)} %bitcast.27, s32[64,128]{1,0:T(8,128)S(1)} %bitcast.28, ...), custom_call_target="tpu_custom_call" | custom-call | tf_op jit(solution)/shard_map/visibilities/pallas_call | solution.py:140
  50.9 8.0 %all_to_all.33 = f32[8,16,128]{2,1,0:T(8,128)S(1)} all-to-all(f32[8,16,128]{2,1,0:T(8,128)S(1)} %bitcast.21), channel_id=1, replica_groups=mesh['vis'=64,'chan'=8] {'chan'}, dimensions={0} | all-to-all | bytes 131072 | tf_op jit(solution)/shard_map/dirty_cells/all_to_all | solution.py:266
  58.9 0.8 %collect.1 = f32[512,128]{1,0:T(8,128)S(1)} custom-call(s32[8,16]{1,0:T(8,128)S(1)} %bitcast.26, f32[128,128]{1,0:T(8,128)S(1)} %bitcast.20), custom_call_target="tpu_custom_call" | custom-call | tf_op jit(solution)/shard_map/collect/pallas_call | solution.py:210
  59.7 18.5 %all_to_all.34.parts_ref = f32[64,8,128]{2,1,0:T(8,128)S(1)} all-to-all(f32[64,8,128]{2,1,0:T(8,128)S(1)} %bitcast.18), channel_id=1, replica_groups=mesh['vis'=64,'chan'=8] {'vis'}, dimensions={0} | all-to-all | bytes 524288 | tf_op jit(solution)/shard_map/owners/all_to_all | solution.py:269
  78.1 0.7 finish.1
  (5 shorter events, 0.0 us)
Async XLA Ops:
  2.0 17.3 %copy-start.8 = (s32[1,1,16]{2,1,0:T(1,128)S(1)}, s32[1,1,16]{2,1,0:T(1,128)}, u32[]{:S(2)}) copy-start(s32[1,1,16]{2,1,0:T(1,128)} %param.14) | copy-start | bytes 196
  2.0 29.8 %copy-start.2 = (f32[64,16]{1,0:T(8,128)S(1)}, f32[64,16]{1,0:T(8,128)}, u32[]{:S(2)}) copy-start(f32[64,16]{1,0:T(8,128)} %constant.4.clone.phase_ref) | copy-start | bytes 12292
  2.0 29.8 %all-to-all-start = ((f32[64,8,128]{2,1,0:T(8,128)}), f32[64,8,128]{2,1,0:T(8,128)S(1)}, u32[]{:S(2)}, u32[]{:S(2)}) async-start(f32[64,8,128]{2,1,0:T(8,128)} %broadcast_in_dim.8), calls=%async_computation | async-start | bytes 524288 | tf_op jit(solution)/shard_map/spread_model/all_to_all | solution.py:248
  19.3 12.5 %copy-start.7 = (f32[2,32,8]{1,2,0:T(8,128)S(1)}, f32[2,32,8]{1,2,0:T(8,128)}, u32[]{:S(2)}) copy-start(f32[2,32,8]{1,2,0:T(8,128)} %param.11) | copy-start | bytes 6148
  31.9 13.5 %copy-start.3 = (s32[1,8192]{1,0:T(1,128)S(1)}, s32[1,8192]{1,0:T(1,128)}, u32[]{:S(2)}) copy-start(s32[1,8192]{1,0:T(1,128)} %param.15) | copy-start | bytes 98308
  31.9 13.5 %copy-start.4 = (s32[1,8192]{1,0:T(1,128)S(1)}, s32[1,8192]{1,0:T(1,128)}, u32[]{:S(2)}) copy-start(s32[1,8192]{1,0:T(1,128)} %param.16) | copy-start | bytes 98308
  31.9 13.5 %copy-start.5 = (f32[1,8192]{1,0:T(1,128)S(1)}, f32[1,8192]{1,0:T(1,128)}, u32[]{:S(2)}) copy-start(f32[1,8192]{1,0:T(1,128)} %param.13) | copy-start | bytes 98308
  31.9 13.5 %copy-start.6 = (f32[2,32,128]{2,1,0:T(8,128)S(1)}, f32[2,32,128]{2,1,0:T(8,128)}, u32[]{:S(2)}) copy-start(f32[2,32,128]{2,1,0:T(8,128)} %constant.5.clone.phase_ref) | copy-start | bytes 98308
  32.9 12.5 %copy-start = (s32[2,1,8192]{2,1,0:T(1,128)S(1)}, s32[2,1,8192]{2,1,0:T(1,128)}, u32[]{:S(2)}) copy-start(s32[2,1,8192]{2,1,0:T(1,128)} %param.17) | copy-start | bytes 196612
  32.9 12.5 %copy-start.1 = (f32[2,1,8192]{2,1,0:T(1,128)S(1)}, f32[2,1,8192]{2,1,0:T(1,128)}, u32[]{:S(2)}) copy-start(f32[2,1,8192]{2,1,0:T(1,128)} %param.12) | copy-start | bytes 196612
